TPU v7x, 32 devices: a whole 2x2x4 slice. The times are simulated.
32 devices in a mesh: seq: 16 (over z, y, x), head: 2 (over core).
Axes of the slice: x: 2, y: 2, z: 4, core: 2. Of those that a mesh axis runs over, the one named last changes fastest.
Arguments:
- block_input: bfloat16 [12, 1024, 1024], P(None, 'seq'), may hold values from -6 to 6
- seq_lengths: int32 [12], replicated, may hold values from 128 to 1024, as said below
- attn_gain: float32 [1024], replicated, may hold values from 0.5 to 1.5
- query_heads: bfloat16 [1024, 96], P(None, 'head'), may hold values from -1 to 1
- query_basis: bfloat16 [1024, 384], replicated, may hold values from -0.1875 to 0.1875
- key_heads: bfloat16 [1024, 32], P(None, 'head'), may hold values from -0.1875 to 0.1875
- key_basis: bfloat16 [1024, 128], replicated, may hold values from -0.1875 to 0.1875
- value_heads: bfloat16 [1024, 32], P(None, 'head'), may hold values from -0.1875 to 0.1875
- value_basis: bfloat16 [1024, 128], replicated, may hold values from -0.1875 to 0.1875
- out_project: bfloat16 [1024, 1024], P('head'), may hold values from -1.5 to 1.5
- ffn_gain: float32 [1024], replicated, may hold values from 0.5 to 1.5
- gate_weight: bfloat16 [1024, 2816], P(None, 'head'), may hold values from -0.1875 to 0.1875
- up_weight: bfloat16 [1024, 2816], P(None, 'head'), may hold values from -0.1875 to 0.1875
- down_weight: bfloat16 [2816, 1024], P('head'), may hold values from -0.109375 to 0.109375
- out_cotangent: bfloat16 [12, 1024, 1024], P(None, 'seq'), may hold values from -6 to 6
Outputs:
- block_output: bfloat16 [12, 1024, 1024], P(None, 'seq')
- input_grad: float32 [12, 1024, 1024], P(None, 'seq')
- attn_gain_grad: float32 [1024], replicated
- query_heads_grad: float32 [1024, 96], P(None, 'head')
- query_basis_grad: float32 [1024, 384], replicated
- key_heads_grad: float32 [1024, 32], P(None, 'head')
- key_basis_grad: float32 [1024, 128], replicated
- value_heads_grad: float32 [1024, 32], P(None, 'head')
- value_basis_grad: float32 [1024, 128], replicated
- out_project_grad: float32 [1024, 1024], P('head')
- ffn_gain_grad: float32 [1024], replicated
- gate_grad: float32 [1024, 2816], P(None, 'head')
- up_grad: float32 [1024, 2816], P(None, 'head')
- down_grad: float32 [2816, 1024], P('head')
Inputs may be any that keep to these rules, and one draw needn't show every extreme that they name: `seq_lengths`: at least one row, drawn from the seed, has the full length 1024.
All inputs are finite; a program needn't handle non-finite values.
Results may differ from a plain program's by a relative error of at most 0.025.
The roundings to bfloat16 on the way count: a program that leaves them out, or rounds other values in their place, can miss the bound.
Values may be sent and summed in bfloat16 or wider, within the bound.
A program may use at most 384 MiB of HBM per device.

v0:
```python
import functools
import math

import jax
import jax.numpy as jnp
from jax import lax
from jax.experimental import pallas as pl
from jax.experimental.pallas import tpu as pltpu
from jax.sharding import PartitionSpec as P

DH = 64
RQ = 6
RK = 2
RV = 2
LANES = 128
EPS = 1e-06
KEY_BLOCK = 256
F32 = jnp.float32
BF16 = jnp.bfloat16


def dot(a, b):
    return lax.dot_general(a, b, (((1,), (0,)), ((), ())), preferred_element_type=F32)


def dot_nt(a, b):
    return lax.dot_general(a, b, (((1,), (1,)), ((), ())), preferred_element_type=F32)


def dot_tn(a, b):
    return lax.dot_general(a, b, (((0,), (0,)), ((), ())), preferred_element_type=F32)


def lane_of(shape):
    return lax.broadcasted_iota(jnp.int32, shape, len(shape) - 1)


def both_halves(pair):
    swapped = pltpu.roll(pair, DH, 1)
    low = lane_of(pair.shape) < DH
    return jnp.where(low, pair, swapped), jnp.where(low, swapped, pair)


def turn(pair, cos, sin):
    half = DH // 2
    first = lane_of(pair.shape) % DH < half
    other = jnp.where(first, pltpu.roll(pair, LANES - half, 1), pltpu.roll(pair, half, 1))
    return pair * cos + other * sin


def split_heads(rows, head_rows, tokens):
    group = lane_of(rows.shape) // DH
    return jnp.concatenate([jnp.where(group == h, rows, jnp.zeros_like(rows)) for h in range(head_rows)], axis=0)


def join_heads(block, head_rows, tokens):
    out = block[:tokens]
    group = lane_of(out.shape) // DH
    for h in range(1, head_rows):
        out = jnp.where(group == h, block[h * tokens : (h + 1) * tokens], out)
    return out


def query_rows(aq, bq, eq_ref, hd):
    aq_high = aq.astype(BF16)
    aq_low = (aq - aq_high.astype(F32)).astype(BF16)
    total = [None] * (hd // LANES)
    for p in range(RQ // 2):
        for half, vec in enumerate(both_halves(bq[:, p * LANES : (p + 1) * LANES])):
            spread = eq_ref[:, (2 * p + half) * hd : (2 * p + half + 1) * hd]
            coef = dot(aq_high, spread) + dot(aq_low, spread)
            for c in range(hd // LANES):
                term = coef[:, c * LANES : (c + 1) * LANES] * vec
                total[c] = term if total[c] is None else total[c] + term
    return [((t / RQ).astype(BF16).astype(F32) * (1.0 / math.sqrt(DH))).astype(BF16) for t in total]


def factor_kernel(width, with_queries, x_ref, gain_ref, wqh_ref, wqb_ref, wkb_ref, wvb_ref, wkh_ref, wvh_ref, cos_ref, sin_ref,
                  eq_ref, xn_ref, aq_ref, bq_ref, kv_ref, hd_ref, *q_refs):
    rows, tokens, model = x_ref.shape
    count = rows * tokens
    x = x_ref[...].astype(F32).reshape(count, model)
    scale = lax.rsqrt(jnp.mean(x * x, axis=-1, keepdims=True) + EPS)
    xn = (x * scale * gain_ref[...]).astype(BF16)
    xn_ref[...] = xn.reshape(rows, tokens, model)
    cos = jnp.concatenate([cos_ref[...]] * rows, axis=0)
    sin = jnp.concatenate([sin_ref[...]] * rows, axis=0)
    keys = turn(dot(xn, wkb_ref[...]), cos, sin).astype(BF16)
    values = dot(xn, wvb_ref[...]).astype(BF16)
    coefs = [dot_nt(xn, w_ref[...]).astype(BF16) for w_ref in (wkh_ref, wvh_ref)]
    pack = jnp.zeros((tokens, LANES), F32)
    for r in range(rows):
        part = slice(r * tokens, (r + 1) * tokens)
        kv_ref[2 * r] = keys[part]
        kv_ref[2 * r + 1] = values[part]
        at = r * width
        for coef in coefs:
            n = coef.shape[1]
            to = lane_of((n, LANES)) == lax.broadcasted_iota(jnp.int32, (n, LANES), 0) + at
            pack = pack + dot(coef[part], jnp.where(to, 1.0, 0.0).astype(BF16))
            at += n
    hd_ref[0] = pack.astype(BF16)
    aq = dot_nt(xn, wqh_ref[...])
    aq_ref[...] = aq.reshape(rows, tokens, aq.shape[1])
    basis = dot(xn, wqb_ref[...])
    bq = jnp.concatenate([turn(basis[:, p : p + LANES], cos, sin) for p in range(0, RQ * DH, LANES)], axis=1)
    bq_ref[...] = bq.reshape(rows, tokens, RQ * DH)
    if with_queries:
        for c, q in enumerate(query_rows(aq, bq, eq_ref, q_refs[0].shape[2])):
            q_refs[0][:, :, c * LANES : (c + 1) * LANES] = q.reshape(rows, tokens, LANES)


def whole(*shape):
    return pl.BlockSpec(shape, lambda *_: (0,) * len(shape))


def factors(x, gain, wqh, wqb, wkb, wvb, wkh, wvh, cos, sin, eq, pack_rows, width, with_queries):
    rows, tokens, model = x.shape
    hd = eq.shape[1] // RQ
    packs = rows // pack_rows
    nq = wqh.shape[0]

    def row_block(last):
        return pl.BlockSpec((pack_rows, tokens, last), lambda g: (g, 0, 0))

    out_specs = [row_block(model), row_block(nq), row_block(RQ * DH),
                 pl.BlockSpec((2 * pack_rows, tokens, LANES), lambda g: (g, 0, 0)),
                 pl.BlockSpec((1, tokens, LANES), lambda g: (g, 0, 0))]
    out_shape = [
        jax.ShapeDtypeStruct((rows, tokens, model), BF16),
        jax.ShapeDtypeStruct((rows, tokens, nq), F32),
        jax.ShapeDtypeStruct((rows, tokens, RQ * DH), F32),
        jax.ShapeDtypeStruct((2 * rows, tokens, LANES), BF16),
        jax.ShapeDtypeStruct((packs, tokens, LANES), BF16),
    ]
    if with_queries:
        out_specs.append(row_block(hd))
        out_shape.append(jax.ShapeDtypeStruct((rows, tokens, hd), BF16))
    return pl.pallas_call(
        functools.partial(factor_kernel, width, with_queries),
        grid=(packs,),
        in_specs=[row_block(model), whole(1, model), *[whole(*w.shape) for w in (wqh, wqb, wkb, wvb, wkh, wvh, cos, sin, eq)]],
        out_specs=out_specs,
        out_shape=out_shape,
        compiler_params=pltpu.CompilerParams(vmem_limit_bytes=32 * 2**20),
        name="factors",
    )(x, gain.reshape(1, model), wqh, wqb, wkb, wvb, wkh, wvh, cos, sin, eq)


def query_grad_rows(dq, aq, bq, eq_ref, cos, sin):
    hd = dq.shape[1]
    aq_high = aq.astype(BF16)
    aq_low = (aq - aq_high.astype(F32)).astype(BF16)
    da = jnp.zeros(aq.shape, F32)
    low = lane_of((dq.shape[0], LANES)) < DH
    turned = []
    for p in range(RQ // 2):
        sums = []
        for half, vec in enumerate(both_halves(bq[:, p * LANES : (p + 1) * LANES])):
            spread = eq_ref[:, (2 * p + half) * hd : (2 * p + half + 1) * hd]
            coef = dot(aq_high, spread) + dot(aq_low, spread)
            acc = None
            prods = []
            for c in range(hd // LANES):
                part = dq[:, c * LANES : (c + 1) * LANES]
                term = coef[:, c * LANES : (c + 1) * LANES] * part
                acc = term if acc is None else acc + term
                prods.append(part * vec)
            prod = jnp.concatenate(prods, axis=1)
            high = prod.astype(BF16)
            rest = (prod - high.astype(F32)).astype(BF16)
            da = da + dot_nt(high, spread) + dot_nt(rest, spread)
            sums.append(acc + pltpu.roll(acc, DH, 1))
        turned.append(turn(jnp.where(low, sums[0], sums[1]), cos, -sin) * (1.0 / RQ))
    return (da * (1.0 / RQ)).astype(BF16), jnp.concatenate(turned, axis=1).astype(BF16)


def query_grad_kernel(dq_ref, aq_ref, bq_ref, eq_ref, cos_ref, sin_ref, da_ref, db_ref):
    rows, tokens, hd = dq_ref.shape
    count = rows * tokens
    da, db = query_grad_rows(
        dq_ref[...].reshape(count, hd), aq_ref[...].reshape(count, -1), bq_ref[...].reshape(count, -1), eq_ref,
        jnp.concatenate([cos_ref[...]] * rows, axis=0), jnp.concatenate([sin_ref[...]] * rows, axis=0))
    da_ref[...] = da.reshape(da_ref.shape)
    db_ref[...] = db.reshape(db_ref.shape)


def query_grads(dq, aq, bq, eq, cos, sin, pack_rows):
    rows, tokens, hd = dq.shape
    nq = aq.shape[2]

    def row_block(last):
        return pl.BlockSpec((pack_rows, tokens, last), lambda g: (g, 0, 0))

    return pl.pallas_call(
        query_grad_kernel,
        grid=(rows // pack_rows,),
        in_specs=[row_block(hd), row_block(nq), row_block(RQ * DH), whole(*eq.shape), whole(*cos.shape), whole(*sin.shape)],
        out_specs=[row_block(nq), row_block(RQ * DH)],
        out_shape=[jax.ShapeDtypeStruct((rows, tokens, nq), BF16), jax.ShapeDtypeStruct((rows, tokens, RQ * DH), BF16)],
        compiler_params=pltpu.CompilerParams(vmem_limit_bytes=56 * 2**20),
        name="query_grads",
    )(dq, aq, bq, eq, cos, sin)


def key_rows(basis):
    turned = basis.astype(F32).T * 0.5
    return turned[:DH], turned[DH:]


def build_heads(coefs, first, second, head_count):
    return jnp.concatenate(
        [coefs[2 * h : 2 * h + 1] * first + coefs[2 * h + 1 : 2 * h + 2] * second for h in range(head_count)], axis=0
    ).astype(BF16)


def row_limits(info_ref, row, tokens, block, lanes):
    first = info_ref[info_ref.shape[0] - 1]
    length = info_ref[row]
    used = jnp.minimum(length, first + tokens)
    slot = lax.broadcasted_iota(jnp.int32, (lanes, 1), 0) % tokens
    return jnp.minimum(first + slot, length - 1), (used + block - 1) // block


def forward_row(q, read, place, width, limit, blocks, block, group, ct_ref):
    tokens, hd = q.shape
    head_count = hd // DH
    lanes = group * tokens
    wide = group * DH
    groups = hd // wide
    queries = [split_heads(q[:, g * wide : (g + 1) * wide], group, tokens) for g in range(groups)]

    def one(b, carry):
        ct_ref[...] = read(2, b).astype(F32).T
        coefs = ct_ref[pl.ds(place, width), :]
        keys = build_heads(coefs[: RK * head_count], *key_rows(read(0, b)), head_count)
        values = build_heads(coefs[RK * head_count :], *key_rows(read(1, b)), head_count)
        live = b * block + lax.broadcasted_iota(jnp.int32, (1, block), 1) <= limit
        out = []
        for g in range(groups):
            peak, total, mixed = carry[g]
            raw = jnp.where(live, dot(queries[g], keys[g * wide : (g + 1) * wide]), -1e30)
            top = jnp.maximum(peak, jnp.max(raw, axis=1, keepdims=True))
            e = jnp.exp(raw - top)
            keep = jnp.exp(peak - top)
            total = total * keep + jnp.sum(e, axis=1, keepdims=True)
            mixed = mixed * keep + dot_nt(e.astype(BF16), values[g * wide : (g + 1) * wide])
            out.append((top, total, mixed))
        return tuple(out)

    start = (jnp.full((lanes, 1), -1e30, F32), jnp.zeros((lanes, 1), F32), jnp.zeros((lanes, wide), F32))
    done = lax.fori_loop(0, blocks, one, (start,) * groups)
    lane = lane_of((tokens, LANES))
    lse = jnp.zeros((tokens, LANES), F32)
    parts = []
    for g in range(groups):
        peak, total, mixed = done[g]
        parts.append(join_heads(mixed / total, group, tokens))
        level = peak + jnp.log(total)
        for h in range(group):
            lse = jnp.where(lane == g * group + h, level[h * tokens : (h + 1) * tokens], lse)
    return parts, lse


def attend_kernel(pack_rows, group, block, width, info_ref, q_ref, kv_ref, hd_ref, o_ref, ob_ref, lse_ref, ct_ref):
    row = pl.program_id(0)
    _, tokens, hd = q_ref.shape
    wide = group * DH
    limit, blocks = row_limits(info_ref, row, tokens, block, group * tokens)

    def read(i, b):
        at = pl.ds(pl.multiple_of(b * block, block), block)
        return hd_ref[0, at, :] if i == 2 else kv_ref[i, at, :]

    parts, lse_ref[0] = forward_row(
        q_ref[0], read, pl.multiple_of(row % pack_rows * width, 8), width, limit, blocks, block, group, ct_ref)
    for g, mixed in enumerate(parts):
        o_ref[0, :, g * wide : (g + 1) * wide] = mixed
        ob_ref[0, :, g * wide : (g + 1) * wide] = mixed.astype(BF16)


def attend(info, q, kv, pack_rows, group, block, width):
    rows, tokens, hd = q.shape
    length = kv.shape[1]

    def own(r, i):
        return (r, 0, 0)

    grid_spec = pltpu.PrefetchScalarGridSpec(
        num_scalar_prefetch=1,
        grid=(rows,),
        in_specs=[
            pl.BlockSpec((1, tokens, hd), own),
            pl.BlockSpec((2, length, LANES), lambda r, i: (lax.rem(r + i[rows], rows), 0, 0)),
            pl.BlockSpec((1, length, LANES), lambda r, i: (2 * rows + r // pack_rows, 0, 0)),
        ],
        out_specs=[pl.BlockSpec((1, tokens, hd), own), pl.BlockSpec((1, tokens, hd), own), pl.BlockSpec((1, tokens, LANES), own)],
        scratch_shapes=[pltpu.VMEM((LANES, block), F32)],
    )
    return pl.pallas_call(
        functools.partial(attend_kernel, pack_rows, group, block, width),
        grid_spec=grid_spec,
        out_shape=[
            jax.ShapeDtypeStruct((rows, tokens, hd), F32),
            jax.ShapeDtypeStruct((rows, tokens, hd), BF16),
            jax.ShapeDtypeStruct((rows, tokens, LANES), F32),
        ],
        compiler_params=pltpu.CompilerParams(vmem_limit_bytes=32 * 2**20),
        name="attend",
    )(info, q, kv, kv)


def attend_back_kernel(pack_rows, group, block, width, info_ref, q_ref, kv_ref, hd_ref, o_ref, do_ref, lse_ref,
                       dq_ref, dkv_ref, dhd_ref, dq_acc, ct_ref, dct_ref):
    row = pl.program_id(0)
    _, tokens, hd = q_ref.shape
    head_count = hd // DH
    lanes = group * tokens
    wide = group * DH
    groups = hd // wide
    limit, blocks = row_limits(info_ref, row, tokens, block, lanes)
    place = pl.multiple_of(row % pack_rows * width, 8)
    queries, grads, deltas, levels = [], [], [], []
    for g in range(groups):
        part = slice(g * wide, (g + 1) * wide)
        do = do_ref[0, :, part]
        queries.append(split_heads(q_ref[0, :, part], group, tokens))
        grads.append(split_heads(do, group, tokens))
        weighed = split_heads(do.astype(F32) * o_ref[0, :, part], group, tokens)
        deltas.append(jnp.sum(weighed, axis=1, keepdims=True))
        levels.append(jnp.concatenate([lse_ref[0, :, h : h + 1] for h in range(g * group, (g + 1) * group)], axis=0))
    queries_t = [q.astype(F32).T.astype(BF16) for q in queries]
    grads_t = [g.astype(F32).T.astype(BF16) for g in grads]
    dq_acc[...] = jnp.zeros_like(dq_acc)
    dkv_ref[...] = jnp.zeros_like(dkv_ref)
    dct_ref[...] = jnp.zeros_like(dct_ref)

    @pl.when(row % pack_rows == 0)
    def _():
        dhd_ref[...] = jnp.zeros_like(dhd_ref)

    def factor_grads(grad, coefs, vectors):
        sums, rows = [None, None], []
        for h in range(head_count):
            part = grad[h * DH : (h + 1) * DH]
            for r in range(2):
                term = coefs[2 * h + r : 2 * h + r + 1] * part
                sums[r] = term if h == 0 else sums[r] + term
                rows.append(jnp.sum(part * vectors[r], axis=0, keepdims=True))
        return (jnp.concatenate(sums, axis=0) * 0.5).T.astype(BF16), rows

    def one(b, carry):
        at = pl.ds(pl.multiple_of(b * block, block), block)
        ct_ref[...] = hd_ref[0, at, :].astype(F32).T
        coefs = ct_ref[pl.ds(place, width), :]
        key_coefs, value_coefs = coefs[: RK * head_count], coefs[RK * head_count :]
        key_vectors, value_vectors = key_rows(kv_ref[0, at, :]), key_rows(kv_ref[1, at, :])
        keys = build_heads(key_coefs, *key_vectors, head_count)
        values = build_heads(value_coefs, *value_vectors, head_count)
        live = b * block + lax.broadcasted_iota(jnp.int32, (1, block), 1) <= limit
        dks, dvs = [], []
        for g in range(groups):
            part = slice(g * wide, (g + 1) * wide)
            p = jnp.where(live, jnp.exp(dot(queries[g], keys[part]) - levels[g]), 0.0)
            dp = dot(grads[g], values[part])
            ds = (p * (dp - deltas[g])).astype(BF16)
            dvs.append(dot(grads_t[g], p.astype(BF16)))
            dks.append(dot(queries_t[g], ds))
            dq_acc[g] += dot_nt(ds, keys[part])
        dkv_ref[0, at, :], key_grads = factor_grads(jnp.concatenate(dks, axis=0), key_coefs, key_vectors)
        dkv_ref[1, at, :], value_grads = factor_grads(jnp.concatenate(dvs, axis=0), value_coefs, value_vectors)
        dct_ref[pl.ds(place, width), :] = jnp.concatenate(key_grads + value_grads, axis=0)
        dhd_ref[0, at, :] = (dhd_ref[0, at, :].astype(F32) + dct_ref[...].T).astype(BF16)
        return carry

    lax.fori_loop(0, blocks, one, 0)
    for g in range(groups):
        dq_ref[0, :, g * wide : (g + 1) * wide] = join_heads(dq_acc[g], group, tokens) * (1.0 / math.sqrt(DH))


def attend_back(info, q, kv, o, do, lse, pack_rows, group, block, width):
    rows, tokens, hd = q.shape
    length = kv.shape[1]
    packs = rows // pack_rows

    def place(r, i):
        return (lax.rem(r + i[rows], rows), 0, 0)

    def own(r, i):
        return (r, 0, 0)

    grid_spec = pltpu.PrefetchScalarGridSpec(
        num_scalar_prefetch=1,
        grid=(rows,),
        in_specs=[
            pl.BlockSpec((1, tokens, hd), own),
            pl.BlockSpec((2, length, LANES), place),
            pl.BlockSpec((1, length, LANES), lambda r, i: (2 * rows + r // pack_rows, 0, 0)),
            pl.BlockSpec((1, tokens, hd), own),
            pl.BlockSpec((1, tokens, hd), own),
            pl.BlockSpec((1, tokens, LANES), own),
        ],
        out_specs=[
            pl.BlockSpec((1, tokens, hd), own),
            pl.BlockSpec((2, length, LANES), place),
            pl.BlockSpec((1, length, LANES), lambda r, i: (r // pack_rows, 0, 0)),
        ],
        scratch_shapes=[pltpu.VMEM((hd // (group * DH), group * tokens, group * DH), F32),
                        pltpu.VMEM((LANES, block), F32), pltpu.VMEM((LANES, block), F32)],
    )
    return pl.pallas_call(
        functools.partial(attend_back_kernel, pack_rows, group, block, width),
        grid_spec=grid_spec,
        out_shape=[
            jax.ShapeDtypeStruct((rows, tokens, hd), F32),
            jax.ShapeDtypeStruct((2 * rows, length, LANES), BF16),
            jax.ShapeDtypeStruct((packs, length, LANES), BF16),
        ],
        compiler_params=pltpu.CompilerParams(vmem_limit_bytes=32 * 2**20),
        name="attend_back",
    )(info, q, kv, kv, o, do, lse)


MESH = pl.DeviceIdType.MESH
SIZES = {"z": 4, "y": 2, "x": 2}
STRIDES = {"z": 4, "y": 2, "x": 1}
CORES = 2


def on_known_slice():
    return lax.axis_size("seq") == math.prod(SIZES.values()) and lax.axis_size("head") == CORES


class Links:
    def __init__(self, send_sems, recv_sems):
        self.seq = lax.axis_index("seq")
        self.core = lax.axis_index("head")
        self.at = {d: lax.rem(self.seq // STRIDES[d], SIZES[d]) for d in SIZES}
        self.send_sems, self.recv_sems = send_sems, recv_sems
        self.count = 0
        self.started = []

    def along(self, d, offset):
        there = lax.rem(self.at[d] + offset, SIZES[d])
        return there, (self.seq + (there - self.at[d]) * STRIDES[d], self.core)

    def other_core(self):
        return (self.seq, 1 - self.core)

    def greet(self, core, chips=True):
        barrier = pltpu.get_barrier_semaphore()
        devices = [self.other_core()] if core else []
        if chips:
            devices += [self.along(d, o)[1] for d in SIZES for o in range(1, SIZES[d])]
        for device in devices:
            pl.semaphore_signal(barrier, inc=1, device_id=device, device_id_type=MESH)
        pl.semaphore_wait(barrier, len(devices))

    def send(self, src, dst, device):
        copy = pltpu.make_async_remote_copy(
            src_ref=src, dst_ref=dst, send_sem=self.send_sems.at[self.count], recv_sem=self.recv_sems.at[self.count],
            device_id=device, device_id_type=MESH)
        self.count += 1
        copy.start()
        self.started.append(copy)
        return copy

    def finish(self):
        for copy in self.started:
            copy.wait_send()


def accumulate(acc, slots):
    lead = acc.shape[:-2]

    def body(i, carry):
        at = []
        for size in reversed(lead):
            at.insert(0, lax.rem(i, size))
            i = i // size
        value = acc[(*at, slice(None), slice(None))].astype(F32)
        for o in range(slots.shape[0]):
            value = value + slots[(o, *at, slice(None), slice(None))].astype(F32)
        acc[(*at, slice(None), slice(None))] = value.astype(BF16)
        return carry

    lax.fori_loop(0, math.prod(lead), body, 0)


def scatter_steps(links, order, source, acc, slots, ready):
    fixed = {}
    for k, d in enumerate(order):
        copies = []
        for o in range(1, SIZES[d]):
            there, device = links.along(d, o)
            view = source if k == 0 else acc
            copies.append(links.send(view({**fixed, d: there}), slots[k].at[o - 1], device))
        yield
        if k == 0:
            ready()
        for copy in copies:
            copy.wait_recv()
        fixed[d] = links.at[d]
        accumulate(acc(fixed), slots[k])


def gather_steps(links, order, out, first):
    for k in reversed(range(len(order))):
        fixed = {d: links.at[d] for d in order[: k + 1]}
        copies = []
        for o in range(1, SIZES[order[k]]):
            _, device = links.along(order[k], o)
            src = first if first is not None and k == len(order) - 1 else out(fixed)
            copies.append(links.send(src, out(fixed), device))
        yield
        for copy in copies:
            copy.wait_recv()


def run_waves(groups):
    live, waiting = [], list(groups)
    while live or waiting:
        if waiting:
            live.append(list(waiting.pop(0)))
        for group in live:
            group[:] = [job for job in group if next(job, "end") != "end"]
        live = [group for group in live if group]


def in_pairs(jobs):
    half = (len(jobs) + 1) // 2
    return [jobs[i : i + 1] + jobs[half + i : half + i + 1] for i in range(half)]


def slot_shapes(order, units, tail):
    shapes, open_dims = [], list(SIZES)
    for d in order:
        open_dims.remove(d)
        shapes.append((SIZES[d] - 1, *units, *[SIZES[e] for e in open_dims], *tail))
    return shapes


def pick(ref, lead, sel, axes, tail=()):
    return ref.at[(*lead, *[sel.get(d, slice(None)) for d in axes], *tail)]


ZYX = ("z", "y", "x")


def collect_jobs(rows, packs):
    step = 1
    own = [(rows + u, min(step, rows - u)) for u in range(0, rows, step)]
    jobs = own + [(2 * rows, packs)]
    half = (len(jobs) + 1) // 2
    return [(first, n, ("y", "x", "z") if i < half else ("x", "y", "z")) for i, (first, n) in enumerate(jobs)]


def collect_groups(rows, packs):
    half = rows // CORES
    lots = [[0]] + [list(range(j, min(j + 2, half))) for j in range(1, half, 2)]
    return [([(2 * rows, packs)] if i == 0 else []) + [(rows + 2 * j, 2) for j in lot] for i, lot in enumerate(lots)], lots


def collect_kernel(pack_rows, group, block, width, len_ref, kv_ref, hd_ref, aq_ref, bq_ref, eq_ref, out_ref, o_ref, ob_ref, lse_ref,
                   q_ref, all_ref, ct_ref, local_sems, out_sems, send_sems, recv_sems):
    rows, tokens, hd = q_ref.shape
    packs = hd_ref.shape[0]
    half = rows // CORES
    wide = group * DH
    planes = block // (SIZES["y"] * SIZES["x"] * tokens)
    links = Links(send_sems, recv_sems)
    own = tuple(links.at[d] for d in ZYX)
    first_slot = links.seq * tokens
    blocks = (first_slot + tokens + block - 1) // block
    groups, lots = collect_groups(rows, packs)
    jobs = [job for lot in groups for job in lot]
    loads = []
    for i, (first, n) in enumerate(jobs):
        src = hd_ref if first == 2 * rows else kv_ref.at[pl.ds(links.core * rows + first - rows, n)]
        loads.append(pltpu.make_async_copy(src, all_ref.at[(pl.ds(first, n), *own)], local_sems.at[i]))
        loads[-1].start()
    links.greet(core=True)
    stores = []

    def keep(first, n):
        store = pltpu.make_async_copy(all_ref.at[pl.ds(first, n)], out_ref.at[pl.ds(first, n)], out_sems.at[len(stores)])
        store.start()
        stores.append(store)

    def job(i, first, n):
        order = ("x", "y", "z") if i % 2 else ("y", "x", "z")
        loads[i].wait()
        yield from gather_steps(links, order, lambda sel: pick(all_ref, [pl.ds(first, n)], sel, ZYX), None)
        if first < 2 * rows:
            copy = links.send(all_ref.at[pl.ds(first, n)], all_ref.at[pl.ds(first - rows, n)], links.other_core())
        keep(first, n)
        if first < 2 * rows:
            yield
            copy.wait_recv()
            keep(first - rows, n)

    def attend_rows(mine, lot):
        def body(i, carry):
            j = lot[0] + i
            row = j + half * (links.core if mine else 1 - links.core)
            unit = rows * mine + 2 * j
            slot = lax.broadcasted_iota(jnp.int32, (group * tokens, 1), 0) % tokens
            limit = jnp.minimum(first_slot + slot, len_ref[row] - 1)
            pack = row // pack_rows
            place = pl.multiple_of((row - pack * pack_rows) * width, 8)

            def read(k, b):
                at = 2 * rows + pack if k == 2 else unit + k
                return all_ref[at, pl.ds(b * planes, planes)].reshape(block, LANES)

            parts, lse_ref[row] = forward_row(q_ref[row], read, place, width, limit, blocks, block, group, ct_ref)
            for g, mixed in enumerate(parts):
                o_ref[row, :, g * wide : (g + 1) * wide] = mixed
                ob_ref[row, :, g * wide : (g + 1) * wide] = mixed.astype(BF16)
            return carry

        lax.fori_loop(0, len(lot), body, 0)

    live, started, wave, i = [], 0, 0, 0
    steps = 3
    while started < len(groups) or live:
        if started < len(groups):
            for first, n in groups[started]:
                live.append(job(i, first, n))
                i += 1
            started += 1
        live[:] = [made for made in live if next(made, "end") != "end"]
        if 0 <= wave - steps - 1 < len(lots):
            attend_rows(0, lots[wave - steps - 1])
        if 0 <= wave - steps < len(lots):
            attend_rows(1, lots[wave - steps])
        if wave < packs:
            part = pl.ds(wave * pack_rows, pack_rows)
            flat = pack_rows * tokens
            made = query_rows(aq_ref[part].reshape(flat, -1), bq_ref[part].reshape(flat, -1), eq_ref, hd)
            for c, q in enumerate(made):
                q_ref[part, :, c * LANES : (c + 1) * LANES] = q.reshape(pack_rows, tokens, LANES)
        wave += 1
    for store in stores:
        store.wait()
    links.finish()


def collect(lengths, kv, hd, aq, bq, eq, pack_rows, group, width):
    units, tokens, _ = kv.shape
    packs = hd.shape[0]
    rows = units // 2
    hidden = (rows, tokens, eq.shape[1] // RQ)
    length = tokens * math.prod(SIZES.values())
    block = length // 2
    count = sum(len(lot) for lot in collect_groups(rows, packs)[0])
    full = (units + packs, *[SIZES[d] for d in ZYX], tokens, LANES)
    vmem, any_space = pl.BlockSpec(memory_space=pltpu.VMEM), pl.BlockSpec(memory_space=pl.ANY)
    out, o, ob, lse, q = pl.pallas_call(
        functools.partial(collect_kernel, pack_rows, group, block, width),
        out_shape=[jax.ShapeDtypeStruct(full, BF16), jax.ShapeDtypeStruct(hidden, F32), jax.ShapeDtypeStruct(hidden, BF16),
                   jax.ShapeDtypeStruct((rows, tokens, LANES), F32), jax.ShapeDtypeStruct(hidden, BF16)],
        in_specs=[pl.BlockSpec(memory_space=pltpu.SMEM), any_space, any_space, vmem, vmem, vmem],
        out_specs=[any_space, vmem, vmem, vmem, vmem],
        scratch_shapes=[pltpu.VMEM(full, BF16), pltpu.VMEM((LANES, block), F32), pltpu.SemaphoreType.DMA((count,)),
                        pltpu.SemaphoreType.DMA((2 * count,)), pltpu.SemaphoreType.DMA((8 * count,)),
                        pltpu.SemaphoreType.DMA((8 * count,))],
        compiler_params=pltpu.CompilerParams(collective_id=1, has_side_effects=True, vmem_limit_bytes=32 * 2**20),
        name="collect",
    )(lengths, kv, hd, aq, bq, eq)
    return out.reshape(units + packs, length, LANES), o, ob, lse, q


def return_kernel(rows, packs, chunk, groups, count, dkv_ref, dhd_ref, cos_ref, sin_ref, dq_ref, aq_ref, bq_ref, eq_ref, *refs):
    ins, refs = refs[:count], refs[count:]
    (dk_ref, dv_ref, dh_ref, da_ref, db_ref), refs = refs[:5], refs[5:]
    outs, refs = refs[:count], refs[count:]
    acc_ref, core_ref, refs = refs[0], refs[1], refs[2:]
    jobs = collect_jobs(rows, packs)
    slot_refs, refs = refs[: 3 * len(jobs)], refs[3 * len(jobs) :]
    cuts = [cut for group in groups for cut in group]
    cut_accs, cut_slots, refs = refs[: len(cuts)], refs[len(cuts) : 4 * len(cuts)], refs[4 * len(cuts) :]
    local_sems, cut_sems, send_sems, recv_sems = refs
    links = Links(send_sems, recv_sems)
    links.greet(core=True)
    own = tuple(links.at[d] for d in ZYX)
    loads, swaps = [], []
    for i, (first, n, _) in enumerate(jobs):
        heads = first == 2 * rows
        part = pl.ds(first - rows, n)
        if not heads:
            swaps.append(links.send(dkv_ref.at[part], core_ref.at[part], links.other_core()))
        load = pltpu.make_async_copy(dhd_ref if heads else dkv_ref.at[pl.ds(first, n)], acc_ref.at[part], local_sems.at[i])
        load.start()
        loads.append(load)
    cut_loads = [start_load(links, cut, ins[cut.array], cut_accs[i], cut_sems.at[2 * i]) for i, cut in enumerate(cuts)]
    dk_ref[...] = jnp.zeros_like(dk_ref)
    dv_ref[...] = jnp.zeros_like(dv_ref)

    def job(i, first, n, order):
        heads = first == 2 * rows
        part = pl.ds(first - rows, n)
        loads[i].wait()
        if not heads:
            swaps[i].wait_recv()

            def add(j, carry):
                u = first - rows + j // SIZES["z"]
                z = lax.rem(j, SIZES["z"])
                acc_ref[u, z] = (acc_ref[u, z].astype(F32) + core_ref[u, z].astype(F32)).astype(BF16)
                return carry

            lax.fori_loop(0, n * SIZES["z"], add, 0)

        def view(sel):
            return pick(acc_ref, [part], sel, ZYX)

        yield from scatter_steps(links, order, view, view, slot_refs[3 * i : 3 * i + 3], lambda: None)
        for u in range(n):
            piece = acc_ref[(first - rows + u, *own)]
            row = links.core * (rows // 2) + (first - rows + u) // 2
            if heads:
                dh_ref[u] = piece
            elif (first - rows + u) % 2 == 0:
                dk_ref[row] = turn(piece.astype(F32), cos_ref[...], -sin_ref[...]).astype(BF16)
            else:
                dv_ref[row] = piece

    def query_part(first):
        part = pl.ds(first, chunk)
        tokens = dq_ref.shape[1]
        cos = jnp.concatenate([cos_ref[...]] * chunk, axis=0)
        sin = jnp.concatenate([sin_ref[...]] * chunk, axis=0)
        da, db = query_grad_rows(dq_ref[part].reshape(chunk * tokens, -1), aq_ref[part].reshape(chunk * tokens, -1),
                                 bq_ref[part].reshape(chunk * tokens, -1), eq_ref, cos, sin)
        da_ref[part] = da.reshape(chunk, tokens, -1)
        db_ref[part] = db.reshape(chunk, tokens, -1)
        yield

    waves = in_pairs([job(i, *j) for i, j in enumerate(jobs)])
    at = 0
    for wave, group in zip(waves, groups):
        for cut in group:
            wave.insert(0, cut_job(links, cut, ins[cut.array], outs[cut.array], cut_accs[at], cut_slots[3 * at : 3 * at + 3],
                                   cut_loads[at], cut_sems.at[2 * at + 1]))
            at += 1
    for i, first in enumerate(range(0, dq_ref.shape[0], chunk)):
        waves[min(i, len(waves) - 1)].append(query_part(first))
    run_waves(waves)
    links.finish()


def give_back(dkv, dhd, cos, sin, dq, aq, bq, eq, chunk, named):
    units, length, _ = dkv.shape
    packs = dhd.shape[0]
    rows = units // 2
    tokens = length // math.prod(SIZES.values())
    dims = tuple(SIZES[d] for d in ZYX)
    jobs = collect_jobs(rows, packs)
    slots = [pltpu.VMEM(shape, BF16) for _, n, order in jobs for shape in slot_shapes(order, (n,), (tokens, LANES))]
    arrays = {name: pieces(name, w) for name, w in named.items()}
    groups = weight_cuts({name: w.shape for name, w in arrays.items()})
    cuts = [cut for group in groups for cut in group]
    copies = 8 * len(jobs) + 10 * len(cuts)
    vmem, any_space = pl.BlockSpec(memory_space=pltpu.VMEM), pl.BlockSpec(memory_space=pl.ANY)
    outs = pl.pallas_call(
        functools.partial(return_kernel, rows, packs, chunk, groups, len(arrays)),
        out_shape=[
            jax.ShapeDtypeStruct((rows, tokens, LANES), BF16),
            jax.ShapeDtypeStruct((rows, tokens, LANES), BF16),
            jax.ShapeDtypeStruct((packs, tokens, LANES), BF16),
            jax.ShapeDtypeStruct(aq.shape, BF16),
            jax.ShapeDtypeStruct(bq.shape, BF16),
            *[jax.ShapeDtypeStruct(w.shape, BF16) for w in arrays.values()],
        ],
        in_specs=[any_space] * 2 + [vmem] * 6 + [any_space] * len(arrays),
        out_specs=[vmem] * 5 + [any_space] * len(arrays),
        scratch_shapes=[pltpu.VMEM((rows + packs, *dims, tokens, LANES), BF16), pltpu.VMEM((rows, *dims, tokens, LANES), BF16),
                        *slots, *[pltpu.VMEM(cut.acc_shape(), BF16) for cut in cuts],
                        *[pltpu.VMEM(shape, BF16) for cut in cuts for shape in cut.slots()],
                        pltpu.SemaphoreType.DMA((len(jobs),)), pltpu.SemaphoreType.DMA((2 * len(cuts),)),
                        pltpu.SemaphoreType.DMA((copies,)), pltpu.SemaphoreType.DMA((copies,))],
        compiler_params=pltpu.CompilerParams(collective_id=2, has_side_effects=True, vmem_limit_bytes=36 * 2**20),
        name="give_back",
    )(dkv.reshape(units, *dims, tokens, LANES), dhd.reshape(packs, *dims, tokens, LANES), cos, sin, dq, aq, bq, eq,
      *arrays.values())
    return outs[:5], [o.reshape(w.shape) for o, w in zip(outs[5:], named.values())]


def pair_kernel(x_ref, out_ref, got_ref, send_sems, recv_sems):
    links = Links(send_sems, recv_sems)
    links.greet(core=True, chips=False)
    copies = [links.send(x_ref.at[r], got_ref.at[r], links.other_core()) for r in range(x_ref.shape[0])]
    for r, copy in enumerate(copies):
        copy.wait_recv()
        out_ref[r] = (x_ref[r].astype(F32) + got_ref[r].astype(F32)).astype(out_ref.dtype)
    links.finish()


def pair_sum(x, ident):
    parts = 4
    rows, tokens, model = x.shape
    flat = x.reshape(parts, rows * tokens // parts, model)
    return pl.pallas_call(
        pair_kernel,
        out_shape=jax.ShapeDtypeStruct(flat.shape, BF16),
        in_specs=[pl.BlockSpec(memory_space=pltpu.VMEM)],
        out_specs=pl.BlockSpec(memory_space=pltpu.VMEM),
        scratch_shapes=[pltpu.VMEM(flat.shape, BF16), pltpu.SemaphoreType.DMA((parts,)), pltpu.SemaphoreType.DMA((parts,))],
        compiler_params=pltpu.CompilerParams(collective_id=ident, has_side_effects=True, vmem_limit_bytes=32 * 2**20),
        name="pair_sum_%d" % ident,
    )(flat).reshape(x.shape)


class Cut:
    def __init__(self, array, axes, rows, cols, order, lane_dim=None, shared=False):
        self.array, self.axes, self.rows, self.cols = array, axes, rows, cols
        self.order, self.lane_dim, self.shared = order, lane_dim, shared

    def tail(self):
        return (self.rows[1], self.cols[1])

    def view(self, ref, sel, core):
        cols = pl.ds(self.cols[0], self.cols[1])
        if self.lane_dim is not None:
            cols = pl.ds(pl.multiple_of(self.cols[0] + sel[self.lane_dim] * self.cols[1], LANES), self.cols[1])
        lead = [core] if self.shared else []
        return pick(ref, lead, sel, self.axes, (pl.ds(self.rows[0], self.rows[1]), cols))

    def inner(self):
        return tuple(d for d in self.axes if d != self.order[0])

    def acc_shape(self):
        return (*[SIZES[d] for d in self.inner()], *self.tail())

    def slots(self):
        shapes, open_dims = [], list(self.inner())
        for d in self.order:
            if d in open_dims:
                open_dims.remove(d)
            shapes.append((SIZES[d] - 1, *[SIZES[e] for e in open_dims], *self.tail()))
        return shapes


def weight_cuts(shapes):
    a, b, c, d = ("x", "y", "z"), ("y", "x", "z"), ("x", "z", "y"), ("y", "z", "x")
    groups = []
    index = {name: i for i, name in enumerate(shapes)}
    axes = ("x", "y", "z")
    if "down" in shapes:
        n, cols = shapes["down"][2:]
        first = n // 32 * 16
        for rows in ((0, first), (first, n - first)):
            groups.append([Cut(index["down"], ("y", "z"), rows, (0, cols // 4), c, lane_dim="x"),
                           Cut(index["down"], ("x", "z"), rows, (cols // 2, cols // 4), d, lane_dim="y")])
    if "out" in shapes:
        n, cols = shapes["out"][3:]
        for rows in ((0, n // 2), (n // 2, n // 2)):
            groups.append([Cut(index["out"], axes, rows, (0, cols // 2), a), Cut(index["out"], axes, rows, (cols // 2, cols // 2), b)])
    if "small" in shapes:
        m, wide = shapes["small"][3:]
        groups.append([Cut(index["small"], ("y", "z", "x"), (0, m), (0, wide), a)])
    if "basis" in shapes:
        n, cols = shapes["basis"][4:]
        cut = cols // LANES // 2 * LANES
        groups[-1] += [Cut(index["basis"], axes, (0, n), (0, cut), a, shared=True),
                       Cut(index["basis"], axes, (0, n), (cut, cols - cut), b, shared=True)]
    return groups


def pieces(name, w):
    dims = (2, 2, 4)
    chips = math.prod(SIZES.values())
    if name == "basis":
        return w.reshape(CORES, *dims, w.shape[0] // CORES // chips, w.shape[1])
    if name == "down":
        return w.reshape(2, 4, -1, w.shape[1])
    if name == "small":
        return w.reshape(2, 4, 2, -1, LANES)
    return w.reshape(*dims, w.shape[0] // chips, w.shape[1])


def start_load(links, cut, ref, acc, sem):
    if cut.shared:
        return None
    load = pltpu.make_async_copy(cut.view(ref, {cut.order[0]: links.at[cut.order[0]]}, links.core), acc, sem)
    load.start()
    return load


def cut_job(links, cut, in_ref, out_ref, acc_ref, slots, load, store_sem, shared_ref=None):
    def acc(sel):
        return pick(acc_ref, [], sel, cut.inner())

    def source(sel):
        return cut.view(in_ref, sel, links.core)

    def out(sel):
        return cut.view(out_ref, sel, links.core)

    if cut.shared:
        cols = pl.ds(cut.cols[0], cut.cols[1])
        summed = pick(shared_ref, [], {cut.order[0]: links.at[cut.order[0]]}, cut.axes, (slice(None), cols))

        def keep(j, carry):
            p, q = j // acc_ref.shape[1], lax.rem(j, acc_ref.shape[1])
            acc_ref[p, q] = summed[p, q]
            return carry

        lax.fori_loop(0, acc_ref.shape[0] * acc_ref.shape[1], keep, 0)

        def source(sel):
            return pick(shared_ref, [], sel, cut.axes, (slice(None), cols))

    yield from scatter_steps(links, cut.order, source, acc, slots, load.wait if load is not None else lambda: None)
    piece = acc({d: links.at[d] for d in cut.inner()})
    store = pltpu.make_async_copy(piece, out(links.at), store_sem)
    store.start()
    steps = gather_steps(links, cut.order, out, piece)
    next(steps)
    yield
    store.wait()
    yield from steps


def weight_kernel(groups, count, basis, *refs):
    jobs = [cut for group in groups for cut in group]
    ins, outs = refs[:count], refs[count : 2 * count]
    at = 2 * count
    accs = refs[at : at + len(jobs)]
    at += len(jobs)
    slots = refs[at : at + 3 * len(jobs)]
    at += 3 * len(jobs)
    shared_own, shared_got, local_sems, send_sems, recv_sems = refs[at:]
    links = Links(send_sems, recv_sems)
    links.greet(core=True)
    loads = [start_load(links, cut, ins[cut.array], accs[i], local_sems.at[2 * i]) for i, cut in enumerate(jobs)]
    own = pltpu.make_async_copy(ins[basis].at[links.core], shared_own, local_sems.at[2 * len(jobs)])
    own.start()
    swap = links.send(ins[basis].at[1 - links.core], shared_got, links.other_core())

    def first_shared():
        own.wait()
        swap.wait_recv()

        def add(j, carry):
            shape = shared_own.shape
            p, q, r = j // (shape[1] * shape[2]), lax.rem(j // shape[2], shape[1]), lax.rem(j, shape[2])
            shared_own[p, q, r] = (shared_own[p, q, r].astype(F32) + shared_got[p, q, r].astype(F32)).astype(BF16)
            return carry

        lax.fori_loop(0, math.prod(shared_own.shape[:3]), add, 0)
        return
        yield

    made, i, ready = [], 0, False
    for group in groups:
        lot = []
        for cut in group:
            if cut.shared and not ready:
                lot.append(first_shared())
                ready = True
            lot.append(cut_job(links, cut, ins[cut.array], outs[cut.array], accs[i], slots[3 * i : 3 * i + 3], loads[i],
                               local_sems.at[2 * i + 1], shared_own))
            i += 1
        made.append(lot)
    run_waves(made)
    last = links.send(outs[basis].at[links.core], outs[basis].at[links.core], links.other_core())
    last.wait_recv()
    links.finish()


def weight_sums(named):
    arrays = {name: pieces(name, w) for name, w in named.items()}
    groups = weight_cuts({name: w.shape for name, w in arrays.items()})
    jobs = [cut for group in groups for cut in group]
    accs = [pltpu.VMEM(cut.acc_shape(), BF16) for cut in jobs]
    slots = [pltpu.VMEM(shape, BF16) for cut in jobs for shape in cut.slots()]
    copies = 10 * len(jobs) + 4
    any_space = pl.BlockSpec(memory_space=pl.ANY)
    shared = arrays["basis"].shape[1:]
    outs = pl.pallas_call(
        functools.partial(weight_kernel, groups, len(arrays), list(arrays).index("basis")),
        out_shape=[jax.ShapeDtypeStruct(w.shape, BF16) for w in arrays.values()],
        in_specs=[any_space] * len(arrays),
        out_specs=[any_space] * len(arrays),
        scratch_shapes=[*accs, *slots, pltpu.VMEM(shared, BF16), pltpu.VMEM(shared, BF16),
                        pltpu.SemaphoreType.DMA((2 * len(jobs) + 1,)), pltpu.SemaphoreType.DMA((copies,)),
                        pltpu.SemaphoreType.DMA((copies,))],
        compiler_params=pltpu.CompilerParams(collective_id=3, has_side_effects=True, vmem_limit_bytes=48 * 2**20),
        name="weight_sums",
    )(*arrays.values())
    return [o.reshape(w.shape) for o, w in zip(outs, named.values())]


def norm_back(inputs, row_scale, gain_vec, grad_rows):
    weighted = grad_rows * gain_vec
    cubed = row_scale * row_scale * row_scale
    input_part = row_scale * weighted - inputs * cubed * jnp.mean(inputs * weighted, axis=-1, keepdims=True)
    gain_part = jnp.sum(grad_rows * inputs * row_scale, axis=(0, 1))
    return (input_part, gain_part)


def project(activations, weight):
    return jnp.einsum("rsd,de->rse", activations, weight, preferred_element_type=F32)


def back_project(grad_rows, weight):
    return jnp.einsum("rse,de->rsd", grad_rows, weight, preferred_element_type=F32)


def weight_grad(normed, grad_rows):
    return jnp.einsum("rsd,rse->de", normed, grad_rows, preferred_element_type=F32)


def head_sum(partial, ident):
    if on_known_slice():
        return pair_sum(partial.astype(BF16), ident).astype(F32)
    return lax.psum(partial.astype(BF16), "head").astype(F32)


def rms_scale(tensor):
    return lax.rsqrt(jnp.mean(tensor * tensor, axis=-1, keepdims=True) + EPS)


def query_table(head_count):
    hd = head_count * DH
    factor = jnp.arange(head_count * RQ, dtype=jnp.int32)[:, None]
    col = jnp.arange(RQ * hd, dtype=jnp.int32)[None, :]
    return jnp.where(factor == col % hd // DH * RQ + col // hd, 1.0, 0.0).astype(BF16)


def rope_tables(position):
    half = DH // 2
    frequency = jnp.exp(jnp.arange(half).astype(F32) * (-2.0 * math.log(10000.0) / DH))
    angles = position[:, None] * frequency[None, :]
    cos, sin = jnp.cos(angles), jnp.sin(angles)
    return jnp.concatenate([cos] * 4, axis=1), jnp.concatenate([-sin, sin, -sin, sin], axis=1)


def shards(
    block_input,
    seq_lengths,
    attn_gain,
    query_heads,
    query_basis,
    key_heads,
    key_basis,
    value_heads,
    value_basis,
    out_project,
    ffn_gain,
    gate_weight,
    up_weight,
    down_weight,
    out_cotangent,
):
    row_count, slot_count, model_dim = block_input.shape
    head_count = query_heads.shape[1] // RQ
    hd = head_count * DH
    length = slot_count * lax.axis_size("seq")
    first_slot = lax.axis_index("seq") * slot_count
    width = head_count * (RK + RV)
    pack_rows = max(n for n in range(1, row_count + 1) if row_count % n == 0 and n * width <= LANES)
    group = min(4, head_count)
    block = math.gcd(length, KEY_BLOCK)
    query_spread = query_table(head_count)
    cos, sin = rope_tables((first_slot + jnp.arange(slot_count, dtype=jnp.int32)).astype(F32))
    normed, aq, bq, own_kv, own_heads, *queries = factors(
        block_input, attn_gain, query_heads.T, query_basis, key_basis, value_basis, key_heads.T, value_heads.T, cos, sin,
        query_spread, pack_rows, width, not on_known_slice())
    inputs = block_input.astype(F32)
    scale_one = rms_scale(inputs)
    shift = (1 - lax.axis_index("head")) * (row_count // CORES) if on_known_slice() else jnp.zeros((), jnp.int32)
    info = jnp.stack([*[seq_lengths[r] for r in range(row_count)], shift, first_slot]).astype(jnp.int32)
    if on_known_slice():
        kv, attended, mixed_flat, lse, queries = collect(
            seq_lengths, own_kv, own_heads, aq, bq, query_spread, pack_rows, group, width)
    else:
        (queries,) = queries
        kv = lax.all_gather(jnp.concatenate([own_kv, own_heads], axis=0), "seq", axis=1, tiled=True)
        attended, mixed_flat, lse = attend(info, queries, kv, pack_rows, group, block, width)
    attn_out = head_sum(project(mixed_flat, out_project), 4)
    middle = inputs + attn_out
    scale_two = rms_scale(middle)
    normed_two = (middle * scale_two * ffn_gain).astype(BF16)
    gate_act = project(normed_two, gate_weight)
    up_act = project(normed_two, up_weight)
    sigmoid_gate = jax.nn.sigmoid(gate_act)
    silu_gate = gate_act * sigmoid_gate
    hidden = (silu_gate * up_act).astype(BF16)
    ffn_out = head_sum(project(hidden, down_weight), 5)
    block_output = (middle + ffn_out).astype(BF16)
    cotangent = out_cotangent.astype(F32)
    down_grad = jnp.einsum("rsf,rsd->fd", hidden, out_cotangent, preferred_element_type=F32)
    d_hidden = jnp.einsum("rsd,fd->rsf", out_cotangent, down_weight, preferred_element_type=F32)
    d_gate = (d_hidden * up_act * (sigmoid_gate * (1.0 + gate_act * (1.0 - sigmoid_gate)))).astype(BF16)
    d_up = (d_hidden * silu_gate).astype(BF16)
    gate_grad = weight_grad(normed_two, d_gate)
    up_grad = weight_grad(normed_two, d_up)
    d_normed_two = head_sum(back_project(d_gate, gate_weight) + back_project(d_up, up_weight), 6)
    d_middle_norm, ffn_gain_part = norm_back(middle, scale_two, ffn_gain, d_normed_two)
    d_middle = cotangent + d_middle_norm
    d_branch = d_middle.astype(BF16)
    out_project_grad = jnp.einsum("rsf,rsd->fd", mixed_flat, d_branch, preferred_element_type=F32)
    d_mixed = back_project(d_branch, out_project).astype(BF16)
    d_queries, d_kv, d_heads = attend_back(info, queries, kv, attended, d_mixed, lse, pack_rows, group, block, width)
    packs = row_count // pack_rows
    model_cut = model_dim // 2
    if on_known_slice():
        (dk_basis, dv_basis, d_heads_own, dq_heads, dq_basis), (down_right, out_project_grad) = give_back(
            d_kv, d_heads, cos, sin, d_queries, aq, bq, query_spread, pack_rows,
            {"down": down_grad[:, model_cut:].astype(BF16), "out": out_project_grad.astype(BF16)})
    else:
        dq_heads, dq_basis = query_grads(d_queries, aq, bq, query_spread, cos, sin, pack_rows)
        key_grads = lax.psum_scatter(
            jnp.concatenate([d_kv, d_heads], axis=0), "seq", scatter_dimension=1, tiled=True)
        d_kv_own = key_grads[: 2 * row_count].reshape(row_count, 2, slot_count, LANES)
        half = DH // 2
        pairs = d_kv_own[:, 0].astype(F32).reshape(row_count, slot_count, 2, 2, half)
        u, w = pairs[:, :, :, 0], pairs[:, :, :, 1]
        c, s = cos[None, :, None, :half], sin[None, :, None, half:DH]
        dk_basis = jnp.stack([u * c + w * s, w * c - u * s], axis=3).reshape(row_count, slot_count, LANES).astype(BF16)
        dv_basis = d_kv_own[:, 1]
        d_heads_own = key_grads[2 * row_count :]
    d_heads_own = d_heads_own[:, :, : width * pack_rows].reshape(packs, slot_count, pack_rows, width)
    d_heads_own = jnp.transpose(d_heads_own, (0, 2, 1, 3)).reshape(row_count, slot_count, width)
    dk_heads, dv_heads = d_heads_own[..., : head_count * RK], d_heads_own[..., head_count * RK :]
    d_normed = head_sum(
        back_project(dq_heads, query_heads) + back_project(dq_basis, query_basis)
        + back_project(dk_heads, key_heads) + back_project(dk_basis, key_basis)
        + back_project(dv_heads, value_heads) + back_project(dv_basis, value_basis), 7)
    d_input_norm, attn_gain_part = norm_back(inputs, scale_one, attn_gain, d_normed)
    input_grad = d_middle + d_input_norm
    head_grads = weight_grad(jnp.concatenate([dq_heads, dk_heads, dv_heads], axis=-1), normed)
    basis_grads = weight_grad(normed, jnp.concatenate([dq_basis, dk_basis, dv_basis], axis=-1))
    small = jnp.concatenate([head_grads, attn_gain_part[None], ffn_gain_part[None]], axis=0).astype(BF16)
    if on_known_slice():
        gate_grad, up_grad, down_left = [
            t.astype(F32) for t in lax.psum(tuple(t.astype(BF16) for t in (gate_grad, up_grad, down_grad[:, :model_cut])), "seq")]
        down_grad = jnp.concatenate([down_left, down_right.astype(F32)], axis=1)
        height = small.shape[0]
        wide = model_dim // LANES
        small = jnp.pad(small, ((0, -height % 32), (0, 0)))
        full = small.shape[0]
        small = jnp.transpose(small.reshape(full, wide, LANES), (1, 0, 2))
        small, basis_grads = weight_sums({"small": small, "basis": basis_grads.astype(BF16)})
        small = jnp.transpose(small, (1, 0, 2)).reshape(full, model_dim)
    else:
        sums = lax.psum(tuple(t.astype(BF16) for t in (gate_grad, up_grad, down_grad, out_project_grad, small)), "seq")
        gate_grad, up_grad, down_grad, out_project_grad, small = [t.astype(F32) for t in sums]
        basis_grads = lax.psum(basis_grads, ("seq", "head"))
    nq, nk, nv = head_count * RQ, head_count * RK, head_count * RV
    cuts = (0, nq, nq + nk, nq + nk + nv)
    query_heads_grad, key_heads_grad, value_heads_grad = [small[i:j].astype(F32).T for i, j in zip(cuts, cuts[1:])]
    cuts = (0, RQ * DH, (RQ + RK) * DH, (RQ + RK + RV) * DH)
    query_basis_grad, key_basis_grad, value_basis_grad = [basis_grads[:, i:j].astype(F32) for i, j in zip(cuts, cuts[1:])]
    return (
        block_output,
        input_grad,
        small[nq + nk + nv].astype(F32),
        query_heads_grad,
        query_basis_grad,
        key_heads_grad,
        key_basis_grad,
        value_heads_grad,
        value_basis_grad,
        out_project_grad.astype(F32),
        small[nq + nk + nv + 1].astype(F32),
        gate_grad,
        up_grad,
        down_grad,
    )


def solution(mesh):
    rows = P(None, "seq", None)
    columns, features = P(None, "head"), P("head", None)
    in_specs = (rows, P(), P(), columns, P(), columns, P(), columns, P(), features, P(), columns, columns, features, rows)
    out_specs = (rows, rows, P(), columns, P(), columns, P(), columns, P(), features, P(), columns, columns, features)
    return jax.shard_map(shards, mesh=mesh, in_specs=in_specs, out_specs=out_specs, check_vma=False)
```

profile of v0, /device:TPU:0, one launch (start us, length us, event | category | flops | bytes accessed | tf_op | source)
XLA Modules:
  0.0 412.1 jit_solution(13761310341285388598)
XLA Ops:
  7.7 1.4 copy-done.2
  9.1 1.1 copy-done.14
  10.3 0.9 copy-done.25
  11.2 0.9 copy-done.27
  12.2 0.9 copy-done.34
  13.0 0.8 copy-done.36
  13.8 0.8 copy-done.38
  14.6 0.7 copy-done.40
  15.2 4.4 %factors.1 = (bf16[12,64,1024]{2,1,0:T(8,128)(2,1)S(1)}, f32[12,64,48]{2,1,0:T(8,128)S(1)}, f32[12,64,384]{2,1,0:T(8,128)S(1)}, bf16[24,64,128]{2,1,0:T(8,128)(2,1)S(1)}, bf16[3,64,128]{2,1,0:T(8,128)(2,1)S(1)}) custom-call(bf16[12,64,1024]{2,1,0:T(8,128)(2,1)S(1)} %copy-done.2, f32[1,1024]{1,0:T(1,128)S(1)} %bitcast.178, bf16[48,1024]{1,0:T(8,128)(2,1)S(1)} %bitcast.172, ...), custom_call_target="tpu_custom_call" | custom-call | tf_op jit(solution)/shard_map/factors/pallas_call | solution.py:139
  19.7 1.1 copy-done.20
  20.8 60.0 %collect.1 = (bf16[27,4,2,2,64,128]{5,4,3,2,1,0:T(8,128)(2,1)S(1)}, f32[12,64,512]{2,1,0:T(8,128)S(1)}, bf16[12,64,512]{2,1,0:T(8,128)(2,1)S(1)}, f32[12,64,128]{2,1,0:T(8,128)S(1)}, bf16[12,64,512]{2,1,0:T(8,128)(2,1)S(1)}) custom-call(s32[12]{0:T(128)S(1)} %copy-done.42, bf16[24,64,128]{2,1,0:T(8,128)(2,1)S(1)} %get-tuple-element.36.kv_ref, ...), custom_call_target="tpu_custom_call" | custom-call | tf_op jit(solution)/shard_map/collect/pallas_call | solution.py:659
  80.8 2.8 copy-done.7
  83.7 1.0 convolution_convert_fusion
  84.7 3.6 pair_sum_4.1
  88.4 0.6 multiply_reduce_fusion
  89.0 2.6 fusion.17
  91.7 0.6 multiply_convert_fusion.3
  92.3 1.2 copy-done.51
  93.5 2.6 fusion.23
  96.1 4.6 %multiply_convert_fusion.1 = (bf16[12,64,1408]{2,1,0:T(8,128)(2,1)S(1)}, bf16[12,64,1408]{2,1,0:T(8,128)(2,1)S(1)}, bf16[12,64,1408]{2,1,0:T(8,128)(2,1)S(1)}) fusion(f32[12,64,1408]{2,1,0:T(8,128)S(1)} %fusion.17, f32[12,64,1408]{2,1,0:T(8,128)S(1)} %fusion.23, bf16[12,64,1024]{2,1,0:T(8,128)(2,1)S(1)} %multiply_convert_fusion.3, ...), kind=kOutput, calls=%fused_computation.9 | convolution fusion | flops 2230812672 | bytes 19595264 | tf_op jit(solution)/shard_map/rsd,de->rse/dot_general | solution.py:1005
  100.7 2.4 bitcast_convert_fusion.2
  103.1 1.7 fusion.82
  104.9 4.0 bitcast_convert_fusion.1
  108.9 4.0 bitcast_convert_fusion
  112.9 5.2 %fusion.21 = f32[12,64,1024]{2,1,0:T(8,128)S(1)} fusion(bf16[12,64,1408]{2,1,0:T(8,128)(2,1)} %copy-done.58, bf16[1024,1408]{1,0:T(8,128)(2,1)} %param.27), kind=kOutput, calls=%fused_computation.42 | convolution fusion | flops 2214592512 | bytes 8192000 | tf_op jit(solution)/shard_map/rse,de->rsd/dot_general | solution.py:1009
  118.2 2.6 add_convert_fusion.1
  120.8 3.6 pair_sum_6.1
  124.5 1.7 fusion.10
  126.2 0.2 copy-done.46
  126.4 1.5 fusion.37
  128.0 1.9 convolution_convert_fusion.1.do_ref
  129.9 2.0 bitcast_convert_fusion.4
  131.9 3.2 copy-done.8
  135.1 1.4 copy-done.19
  136.5 1.1 copy-done.30
  137.7 1.1 copy-done.31
  138.8 1.0 copy-done.33
  139.8 21.0 %attend_back.1 = (f32[12,64,512]{2,1,0:T(8,128)S(1)}, bf16[24,1024,128]{2,1,0:T(8,128)(2,1)S(1)}, bf16[3,1024,128]{2,1,0:T(8,128)(2,1)S(1)}) custom-call(s32[14]{0:T(128)S(1)} %pad_add_fusion.info_ref, bf16[12,64,512]{2,1,0:T(8,128)(2,1)S(1)} %copy-done.30, bf16[27,1024,128]{2,1,0:T(8,128)(2,1)S(1)} %bitcast.151, bf16[27,1024,128]{2,1,0:T(8,128)(2,1)S(1)} %bitcast.152, ...), custom_call_target="tpu_custom_call" | custom-call | tf_op jit(solution)/shard_map/attend_back/pallas_call | solution.py:411
  160.9 136.2 %give_back.1 = (bf16[12,64,128]{2,1,0:T(8,128)(2,1)S(1)}, bf16[12,64,128]{2,1,0:T(8,128)(2,1)S(1)}, bf16[3,64,128]{2,1,0:T(8,128)(2,1)S(1)}, bf16[12,64,48]{2,1,...) custom-call(bf16[24,4,2,2,64,128]{5,4,3,2,1,0:T(8,128)(2,1)S(1)} %bi, ...), custom_call_target="tpu_custom_call" | custom-call | tf_op jit(solution)/shard_map/give_back/pallas_call | solution.py:766
  297.3 0.6 fusion.54
  298.0 0.5 fusion.56
  298.5 0.5 fusion.61
  299.1 0.6 fusion.47
  299.7 0.6 fusion.49
  300.3 1.6 add_convert_fusion
  301.9 3.6 pair_sum_7.1
  305.5 2.6 fusion.29
  308.2 3.6 pair_sum_5.1
  311.8 1.4 fusion.15
  313.2 0.5 fusion.34
  313.8 1.4 bitcast_convert_fusion.3
  315.2 47.2 %weight_sums.1 = (bf16[2,4,2,48,128]{4,3,2,1,0:T(8,128)(2,1)S(1)}, bf16[2,2,2,4,32,640]{5,4,3,2,1,0:T(8,128)(2,1)S(1)}) custom-call(bf16[2,4,2,48,128]{4,3,2,1,0:T(8,128)(2,1)S(1)} %bitcast.171, bf16[2,2,2,4,32,640]{5,4,3,2,1,0:T(8,128)(2,1)S(1)} %bitcast.168), custom_call_target="tpu_custom_call" | custom-call | tf_op jit(solution)/shard_map/weight_sums/pallas_call | solution.py:982
  362.5 0.6 copy.67
  363.1 0.6 copy.66
  363.8 0.6 slice_convert_fusion.3
  364.4 0.7 bitcast_bitcast_fusion
  365.1 1.0 slice_convert_fusion.1
  366.1 1.2 slice_convert_fusion
  367.3 1.6 bitcast_convert_fusion.5
  369.0 4.2 %fusion.8 = (f32[12,64,1024]{2,1,0:T(8,128)}, bf16[12,64,1024]{2,1,0:T(8,128)(2,1)}) fusion(bf16[12,64,1024]{2,1,0:T(8,128)(2,1)S(1)} %bitcast.157, bf16[12,64,1024]{2,1,0:T(8,128)(2,1)S(1)} %copy-done.4, f32[12,64]{1,0:T(8,128)S(1)} %broadcast_multiply_fusion, f32[12,64]{1,0:T(8,128)S(1)} %get-tuple-element.83, f32[1024]{0:T(1024)S(1)} %copy-done.41, ...), kind=kLoop, calls=%fused_computation.23 | loop fusion | flops 16515072 | bytes 14182400 | tf_op jit(solution)/shard_map/add | solution.py:1134
  373.2 20.6 %all-reduce.4.cloned.1.call-done = (bf16[1024,1408]{1,0:T(8,128)(2,1)}, bf16[1024,1408]{1,0:T(8,128)(2,1)}, bf16[1408,512]{1,0:T(8,128)(2,1)}) async-done(((bf16[1024,1408]{1,0:T(8,128)(2,1)}, bf16[1024,1408]{1,0:T(8,128)(2,1)}, bf16[1408,512]{1,0:T(8,128)(2,1)}), (bf16[1024,1408]{1,0:T(8,128)(2,1)}, bf16[1024,1408]{1,0:T(8,128)(2,1)}, bf16[1408,512]{1,0:T(8,128)(2,1)})) %all-reduce.4.cloned.1.call-update) | async-done | bytes 7208976 | tf_op jit(solution)/shard_map/psum | solution.py:1140
  393.8 4.9 %convert_element_type.190 = f32[1024,1408]{1,0:T(8,128)} convert(bf16[1024,1408]{1,0:T(8,128)(2,1)} %get-tuple-element.63) | non-fusion elementwise | flops 1441792 | bytes 8650752 | tf_op jit(solution)/shard_map/convert_element_type | solution.py:1140
  398.7 2.9 convert_element_type.192
  401.6 3.3 maximum_convert_fusion
  (124 shorter events, 1.1 us)
Async XLA Ops:
  7.2 88.9 %copy-start = (bf16[1024,1408]{1,0:T(8,128)(2,1)S(1)}, bf16[1024,1408]{1,0:T(8,128)(2,1)}, u32[]{:S(2)}) copy-start(bf16[1024,1408]{1,0:T(8,128)(2,1)} %param.26) | copy-start | bytes 8650756
  7.2 13.6 %copy-start.42 = (s32[12]{0:T(128)S(1)}, s32[12]{0:T(128)}, u32[]{:S(2)}) copy-start(s32[12]{0:T(128)} %len_ref.1) | copy-start | bytes 148
  7.2 386.6 %all-reduce.4.cloned.1.call-start = ((), (), s32[]{:S(2)}) async-start(), calls=%async_computation | async-start | bytes 14417920 | tf_op jit(solution)/shard_map/psum | solution.py:1140
  7.7 1.4 copy-start.2
  9.1 1.1 copy-start.14
  10.2 0.9 copy-start.25
  11.2 0.9 copy-start.27
  12.2 0.9 copy-start.34
  13.0 0.8 copy-start.36
  13.8 0.8 copy-start.38
  14.6 0.7 copy-start.40
  15.2 68.4 %copy-start.54 = (bf16[512,1024]{1,0:T(8,128)(2,1)S(1)}, bf16[512,1024]{1,0:T(8,128)(2,1)}, u32[]{:S(2)}) copy-start(bf16[512,1024]{1,0:T(8,128)(2,1)} %param.24) | copy-start | bytes 3145732
  19.7 1.1 copy-start.20
  20.8 63.9 %copy-start.12 = (f32[12,64,384]{2,1,0:T(8,128)}, f32[12,64,384]{2,1,0:T(8,128)S(1)}, u32[]{:S(2)}) copy-start(f32[12,64,384]{2,1,0:T(8,128)S(1)} %get-tuple-element.39.bq_ref) | copy-start | bytes 3538948
  20.8 63.9 %copy-start.16 = (f32[12,64,48]{2,1,0:T(8,128)}, f32[12,64,48]{2,1,0:T(8,128)S(1)}, u32[]{:S(2)}) copy-start(f32[12,64,48]{2,1,0:T(8,128)S(1)} %get-tuple-element.38.aq_ref) | copy-start | bytes 442372
  80.8 2.8 copy-start.7
  83.7 4.7 %copy-start.18 = (f32[12,64,512]{2,1,0:T(8,128)}, f32[12,64,512]{2,1,0:T(8,128)S(1)}, u32[]{:S(2)}) copy-start(f32[12,64,512]{2,1,0:T(8,128)S(1)} %get-tuple-element.43.o_ref) | copy-start | bytes 4718596
  83.7 4.7 %copy-start.29 = (bf16[12,64,512]{2,1,0:T(8,128)(2,1)}, bf16[12,64,512]{2,1,0:T(8,128)(2,1)S(1)}, u32[]{:S(2)}) copy-start(bf16[12,64,512]{2,1,0:T(8,128)(2,1)S(1)} %get-tuple-element.41.q_ref) | copy-start | bytes 2359300
  83.7 4.7 %copy-start.32 = (f32[12,64,128]{2,1,0:T(8,128)}, f32[12,64,128]{2,1,0:T(8,128)S(1)}, u32[]{:S(2)}) copy-start(f32[12,64,128]{2,1,0:T(8,128)S(1)} %get-tuple-element.44.lse_ref) | copy-start | bytes 1179652
  83.7 4.7 %copy-start.43 = (bf16[12,64,512]{2,1,0:T(8,128)(2,1)}, bf16[12,64,512]{2,1,0:T(8,128)(2,1)S(1)}, u32[]{:S(2)}) copy-start(bf16[12,64,512]{2,1,0:T(8,128)(2,1)S(1)} %get-tuple-element.40) | copy-start | bytes 2359300
  83.7 4.7 %copy-start.3 = (bf16[12,64,1024]{2,1,0:T(8,128)(2,1)S(1)}, bf16[12,64,1024]{2,1,0:T(8,128)(2,1)}, u32[]{:S(2)}) copy-start(bf16[12,64,1024]{2,1,0:T(8,128)(2,1)} %x_ref.1) | copy-start | bytes 4718596
  84.7 4.3 %copy-start.45 = (bf16[12,64,1024]{2,1,0:T(8,128)(2,1)S(1)}, bf16[12,64,1024]{2,1,0:T(8,128)(2,1)}, u32[]{:S(2)}) copy-start(bf16[12,64,1024]{2,1,0:T(8,128)(2,1)} %param.29) | copy-start | bytes 4718596
  84.7 4.3 %copy-start.52 = (bf16[1408,1024]{1,0:T(8,128)(2,1)S(1)}, bf16[1408,1024]{1,0:T(8,128)(2,1)}, u32[]{:S(2)}) copy-start(bf16[1408,1024]{1,0:T(8,128)(2,1)} %param.28) | copy-start | bytes 8650756
  88.4 3.3 copy-start.5
  89.0 2.7 copy-start.50
  91.6 1.8 copy-start.51
  100.7 2.5 copy-start.59
  100.7 4.2 %copy-start.56 = (bf16[12,64,1408]{2,1,0:T(8,128)(2,1)}, bf16[12,64,1408]{2,1,0:T(8,128)(2,1)S(1)}, u32[]{:S(2)}) copy-start(bf16[12,64,1408]{2,1,0:T(8,128)(2,1)S(1)} %get-tuple-element.66) | copy-start | bytes 6488068
  100.7 8.2 %copy-start.58 = (bf16[12,64,1408]{2,1,0:T(8,128)(2,1)}, bf16[12,64,1408]{2,1,0:T(8,128)(2,1)S(1)}, u32[]{:S(2)}) copy-start(bf16[12,64,1408]{2,1,0:T(8,128)(2,1)S(1)} %get-tuple-element.67) | copy-start | bytes 6488068
  112.9 5.3 %copy-start.57 = (bf16[12,64,1408]{2,1,0:T(8,128)(2,1)S(1)}, bf16[12,64,1408]{2,1,0:T(8,128)(2,1)}, u32[]{:S(2)}) copy-start(bf16[12,64,1408]{2,1,0:T(8,128)(2,1)} %copy-done.56) | copy-start | bytes 6488068
  120.8 3.6 copy-start.4
  120.8 3.6 copy-start.6
  124.4 3.5 copy-start.9
  124.5 2.0 copy-start.46
  126.4 1.5 copy-start.55
  128.0 1.9 copy-start.44
  131.9 3.2 copy-start.8
  135.1 1.4 copy-start.19
  136.5 1.1 copy-start.30
  137.7 1.1 copy-start.31
  138.8 1.0 copy-start.33
  139.8 21.1 %copy-start.11 = (bf16[1408,512]{1,0:T(8,128)(2,1)S(1)}, bf16[1408,512]{1,0:T(8,128)(2,1)}, u32[]{:S(2)}) copy-start(bf16[1408,512]{1,0:T(8,128)(2,1)} %get-tuple-element.72) | copy-start | bytes 4325380
  139.8 21.1 %copy-start.13 = (f32[12,64,384]{2,1,0:T(8,128)S(1)}, f32[12,64,384]{2,1,0:T(8,128)}, u32[]{:S(2)}) copy-start(f32[12,64,384]{2,1,0:T(8,128)} %copy-done.12) | copy-start | bytes 3538948
  139.8 21.1 %copy-start.17 = (f32[12,64,48]{2,1,0:T(8,128)S(1)}, f32[12,64,48]{2,1,0:T(8,128)}, u32[]{:S(2)}) copy-start(f32[12,64,48]{2,1,0:T(8,128)} %copy-done.16) | copy-start | bytes 442372
  139.8 21.1 %copy-start.24 = (bf16[512,1024]{1,0:T(8,128)(2,1)S(1)}, bf16[512,1024]{1,0:T(8,128)(2,1)}, u32[]{:S(2)}) copy-start(bf16[512,1024]{1,0:T(8,128)(2,1)} %bitcast_convert_fusion.4) | copy-start | bytes 3145732
  160.9 136.4 %copy-start.37 = (bf16[1024,16]{0,1:T(8,128)(2,1)S(1)}, bf16[1024,16]{0,1:T(8,128)(2,1)}, u32[]{:S(2)}) copy-start(bf16[1024,16]{0,1:T(8,128)(2,1)} %param.22) | copy-start | bytes 98308
  297.1 1.4 copy-start.22
  297.1 0.8 copy-start.39
  297.3 1.2 copy-start.35
  297.9 1.1 copy-start.26
  298.5 1.2 copy-start.28
  299.1 1.2 copy-start.15
  300.3 5.2 %copy-start.60 = (bf16[12,64,1408]{2,1,0:T(8,128)(2,1)S(1)}, bf16[12,64,1408]{2,1,0:T(8,128)(2,1)}, u32[]{:S(2)}) copy-start(bf16[12,64,1408]{2,1,0:T(8,128)(2,1)} %copy-done.59) | copy-start | bytes 6488068
  301.9 3.6 copy-start.53
  308.2 3.7 copy-start.41
  308.2 5.0 %copy-start.21 = (bf16[12,64,1024]{2,1,0:T(8,128)(2,1)S(1)}, bf16[12,64,1024]{2,1,0:T(8,128)(2,1)}, u32[]{:S(2)}) copy-start(bf16[12,64,1024]{2,1,0:T(8,128)(2,1)} %copy-done.20) | copy-start | bytes 4718596
  366.1 2.9 copy-start.10
  366.1 2.9 copy-start.47
  393.8 4.9 %copy-start.48 = (bf16[1024,1408]{1,0:T(8,128)(2,1)S(1)}, bf16[1024,1408]{1,0:T(8,128)(2,1)}, u32[]{:S(2)}) copy-start(bf16[1024,1408]{1,0:T(8,128)(2,1)} %get-tuple-element.64) | copy-start | bytes 8650756
  398.6 2.9 copy-start.23
  398.7 3.0 copy-start.49
  401.6 3.4 copy-start.1
Sparse Core Ops, SparseCore 0:
  113.0 280.7 all-reduce.3
where the time goes:
time: 419 us; the launch traced here: 412 us
  Pallas kernels  283 us (68%)
  matrix products  42 us (10%)
  other arithmetic  26.9 us (6%)
  local copies, waits for them, and re-layouts  24.2 us (6%)
  waiting for transfers between devices  20.6 us (5%)
  between operations  15.1 us (4%)
    pallas_call x1, Pallas kernels, give_back(): pl.pallas_call(functools.partial(return_kernel, rows, packs, chunk, group...  136 us
    pallas_call x1, Pallas kernels, collect(): pl.pallas_call(functools.partial(collect_kernel, pack_rows, group, block,...  60 us
    pallas_call x1, Pallas kernels, weight_sums(): pl.pallas_call(functools.partial(weight_kernel, groups, len(arrays), list...  47.2 us
    unnamed x122, local copies, waits for them, and re-layouts  21.1 us
    pallas_call x1, Pallas kernels, attend_back(): pl.pallas_call(functools.partial(attend_back_kernel, pack_rows, group, bl...  21 us
    psum x1, waiting for transfers between devices, shards(): lax.psum(tuple((t.astype(BF16) for t in (gate_grad, up_grad, down_grad[:,...  20.6 us
    pallas_call x4, Pallas kernels, pair_sum(): pl.pallas_call(pair_kernel, out_shape=jax.ShapeDtypeStruct(flat.shape, BF...  14.4 us
    dot_general x9, matrix products, back_project(): jnp.einsum('rse,de->rsd', grad_rows, weight, preferred_element_type=F32)  14.2 us
  transfers between devices with their start and end apart: 1, of which 1 were waited for; matrix products, arithmetic and copies ran while one was open for 9% of the time, Pallas kernels for 52%

commit v1 on v0

--- a/solution.py
+++ b/solution.py
@@ -853,6 +853,10 @@
         for rows in ((0, first), (first, n - first)):
             groups.append([Cut(index["down"], ("y", "z"), rows, (0, cols // 4), c, lane_dim="x"),
                            Cut(index["down"], ("x", "z"), rows, (cols // 2, cols // 4), d, lane_dim="y")])
+    if "gate" in shapes:
+        n, cols = shapes["gate"][3:]
+        cut = (cols // LANES + 1) // 2 * LANES
+        groups.append([Cut(index["gate"], axes, (0, n), (0, cut), a), Cut(index["gate"], axes, (0, n), (cut, cols - cut), b)])
     if "out" in shapes:
         n, cols = shapes["out"][3:]
         for rows in ((0, n // 2), (n // 2, n // 2)):
@@ -923,10 +927,11 @@
     yield from steps
 
 
-def weight_kernel(groups, count, basis, *refs):
+def weight_kernel(groups, count, basis, small, swapped, *refs):
     jobs = [cut for group in groups for cut in group]
-    ins, outs = refs[:count], refs[count : 2 * count]
-    at = 2 * count
+    ins, mine, refs = refs[:count], refs[count : count + swapped], refs[count + swapped :]
+    outs, theirs, their_small, refs = refs[:count], refs[count : count + swapped], refs[count + swapped], refs[count + swapped + 1 :]
+    at = 0
     accs = refs[at : at + len(jobs)]
     at += len(jobs)
     slots = refs[at : at + 3 * len(jobs)]
@@ -938,6 +943,7 @@
     own = pltpu.make_async_copy(ins[basis].at[links.core], shared_own, local_sems.at[2 * len(jobs)])
     own.start()
     swap = links.send(ins[basis].at[1 - links.core], shared_got, links.other_core())
+    swaps = [links.send(src, dst, links.other_core()) for src, dst in zip(mine, theirs)]
 
     def first_shared():
         own.wait()
@@ -965,32 +971,38 @@
             i += 1
         made.append(lot)
     run_waves(made)
-    last = links.send(outs[basis].at[links.core], outs[basis].at[links.core], links.other_core())
-    last.wait_recv()
+    swaps.append(links.send(outs[basis].at[links.core], outs[basis].at[links.core], links.other_core()))
+    swaps.append(links.send(outs[small], their_small, links.other_core()))
+    for copy in swaps:
+        copy.wait_recv()
     links.finish()
 
 
-def weight_sums(named):
+def weight_sums(named, partials):
     arrays = {name: pieces(name, w) for name, w in named.items()}
+    names = list(arrays)
     groups = weight_cuts({name: w.shape for name, w in arrays.items()})
     jobs = [cut for group in groups for cut in group]
     accs = [pltpu.VMEM(cut.acc_shape(), BF16) for cut in jobs]
     slots = [pltpu.VMEM(shape, BF16) for cut in jobs for shape in cut.slots()]
-    copies = 10 * len(jobs) + 4
+    copies = 10 * len(jobs) + 4 + len(partials)
     any_space = pl.BlockSpec(memory_space=pl.ANY)
     shared = arrays["basis"].shape[1:]
+    shapes = [w.shape for w in (*arrays.values(), *partials, arrays["small"])]
     outs = pl.pallas_call(
-        functools.partial(weight_kernel, groups, len(arrays), list(arrays).index("basis")),
-        out_shape=[jax.ShapeDtypeStruct(w.shape, BF16) for w in arrays.values()],
-        in_specs=[any_space] * len(arrays),
-        out_specs=[any_space] * len(arrays),
+        functools.partial(weight_kernel, groups, len(arrays), names.index("basis"), names.index("small"), len(partials)),
+        out_shape=[jax.ShapeDtypeStruct(shape, BF16) for shape in shapes],
+        in_specs=[any_space] * (len(arrays) + len(partials)),
+        out_specs=[any_space] * len(shapes),
         scratch_shapes=[*accs, *slots, pltpu.VMEM(shared, BF16), pltpu.VMEM(shared, BF16),
                         pltpu.SemaphoreType.DMA((2 * len(jobs) + 1,)), pltpu.SemaphoreType.DMA((copies,)),
                         pltpu.SemaphoreType.DMA((copies,))],
-        compiler_params=pltpu.CompilerParams(collective_id=3, has_side_effects=True, vmem_limit_bytes=48 * 2**20),
+        compiler_params=pltpu.CompilerParams(collective_id=3, has_side_effects=True, vmem_limit_bytes=24 * 2**20),
         name="weight_sums",
-    )(*arrays.values())
-    return [o.reshape(w.shape) for o, w in zip(outs, named.values())]
+    )(*arrays.values(), *partials)
+    count = len(arrays)
+    sums = [o.reshape(w.shape) for o, w in zip(outs, named.values())]
+    return sums, outs[count:-1], outs[-1].reshape(named["small"].shape)
 
 
 def norm_back(inputs, row_scale, gain_vec, grad_rows):
@@ -1089,15 +1101,16 @@
     sigmoid_gate = jax.nn.sigmoid(gate_act)
     silu_gate = gate_act * sigmoid_gate
     hidden = (silu_gate * up_act).astype(BF16)
-    ffn_out = head_sum(project(hidden, down_weight), 5)
-    block_output = (middle + ffn_out).astype(BF16)
+    ffn_part = project(hidden, down_weight).astype(BF16)
     cotangent = out_cotangent.astype(F32)
-    down_grad = jnp.einsum("rsf,rsd->fd", hidden, out_cotangent, preferred_element_type=F32)
     d_hidden = jnp.einsum("rsd,fd->rsf", out_cotangent, down_weight, preferred_element_type=F32)
     d_gate = (d_hidden * up_act * (sigmoid_gate * (1.0 + gate_act * (1.0 - sigmoid_gate)))).astype(BF16)
     d_up = (d_hidden * silu_gate).astype(BF16)
-    gate_grad = weight_grad(normed_two, d_gate)
+    known = on_known_slice()
+    model_cut, gate_cut = (model_dim // 2, model_dim // 4) if known else (model_dim, 0)
+    gate_grad = weight_grad(normed_two[..., gate_cut:], d_gate)
     up_grad = weight_grad(normed_two, d_up)
+    down_grad = weight_grad(hidden, out_cotangent[..., :model_cut])
     d_normed_two = head_sum(back_project(d_gate, gate_weight) + back_project(d_up, up_weight), 6)
     d_middle_norm, ffn_gain_part = norm_back(middle, scale_two, ffn_gain, d_normed_two)
     d_middle = cotangent + d_middle_norm
@@ -1106,11 +1119,12 @@
     d_mixed = back_project(d_branch, out_project).astype(BF16)
     d_queries, d_kv, d_heads = attend_back(info, queries, kv, attended, d_mixed, lse, pack_rows, group, block, width)
     packs = row_count // pack_rows
-    model_cut = model_dim // 2
-    if on_known_slice():
-        (dk_basis, dv_basis, d_heads_own, dq_heads, dq_basis), (down_right, out_project_grad) = give_back(
+    if known:
+        down_right = weight_grad(hidden, out_cotangent[..., model_cut:])
+        gate_top = weight_grad(normed_two[..., :gate_cut], d_gate)
+        (dk_basis, dv_basis, d_heads_own, dq_heads, dq_basis), (down_right, gate_top, out_project_grad) = give_back(
             d_kv, d_heads, cos, sin, d_queries, aq, bq, query_spread, pack_rows,
-            {"down": down_grad[:, model_cut:].astype(BF16), "out": out_project_grad.astype(BF16)})
+            {"down": down_right.astype(BF16), "gate": gate_top.astype(BF16), "out": out_project_grad.astype(BF16)})
     else:
         dq_heads, dq_basis = query_grads(d_queries, aq, bq, query_spread, cos, sin, pack_rows)
         key_grads = lax.psum_scatter(
@@ -1126,30 +1140,42 @@
     d_heads_own = d_heads_own[:, :, : width * pack_rows].reshape(packs, slot_count, pack_rows, width)
     d_heads_own = jnp.transpose(d_heads_own, (0, 2, 1, 3)).reshape(row_count, slot_count, width)
     dk_heads, dv_heads = d_heads_own[..., : head_count * RK], d_heads_own[..., head_count * RK :]
-    d_normed = head_sum(
+    normed_part = (
         back_project(dq_heads, query_heads) + back_project(dq_basis, query_basis)
         + back_project(dk_heads, key_heads) + back_project(dk_basis, key_basis)
-        + back_project(dv_heads, value_heads) + back_project(dv_basis, value_basis), 7)
-    d_input_norm, attn_gain_part = norm_back(inputs, scale_one, attn_gain, d_normed)
-    input_grad = d_middle + d_input_norm
+        + back_project(dv_heads, value_heads) + back_project(dv_basis, value_basis))
+    attn_gain_part = jnp.sum(normed_part * inputs * scale_one, axis=(0, 1))
+    normed_part = normed_part.astype(BF16)
     head_grads = weight_grad(jnp.concatenate([dq_heads, dk_heads, dv_heads], axis=-1), normed)
     basis_grads = weight_grad(normed, jnp.concatenate([dq_basis, dk_basis, dv_basis], axis=-1))
     small = jnp.concatenate([head_grads, attn_gain_part[None], ffn_gain_part[None]], axis=0).astype(BF16)
-    if on_known_slice():
-        gate_grad, up_grad, down_left = [
-            t.astype(F32) for t in lax.psum(tuple(t.astype(BF16) for t in (gate_grad, up_grad, down_grad[:, :model_cut])), "seq")]
-        down_grad = jnp.concatenate([down_left, down_right.astype(F32)], axis=1)
+    gain_at = head_grads.shape[0]
+    if known:
+        gate_grad, up_grad, down_grad = [
+            t.astype(F32) for t in lax.psum(tuple(t.astype(BF16) for t in (gate_grad, up_grad, down_grad)), "seq")]
+        gate_grad = jnp.concatenate([gate_top.astype(F32), gate_grad], axis=0)
+        down_grad = jnp.concatenate([down_grad, down_right.astype(F32)], axis=1)
         height = small.shape[0]
         wide = model_dim // LANES
         small = jnp.pad(small, ((0, -height % 32), (0, 0)))
         full = small.shape[0]
         small = jnp.transpose(small.reshape(full, wide, LANES), (1, 0, 2))
-        small, basis_grads = weight_sums({"small": small, "basis": basis_grads.astype(BF16)})
+        (small, basis_grads), (normed_other, ffn_other), small_other = weight_sums(
+            {"small": small, "basis": basis_grads.astype(BF16)}, (normed_part, ffn_part))
+        attn_gain_grad = (small[:, gain_at].astype(F32) + small_other[:, gain_at].astype(F32)).reshape(model_dim)
         small = jnp.transpose(small, (1, 0, 2)).reshape(full, model_dim)
+        d_normed = normed_part.astype(F32) + normed_other.astype(F32)
+        ffn_out = ffn_part.astype(F32) + ffn_other.astype(F32)
     else:
         sums = lax.psum(tuple(t.astype(BF16) for t in (gate_grad, up_grad, down_grad, out_project_grad, small)), "seq")
         gate_grad, up_grad, down_grad, out_project_grad, small = [t.astype(F32) for t in sums]
+        attn_gain_grad = lax.psum(small[gain_at].astype(BF16), "head").astype(F32)
         basis_grads = lax.psum(basis_grads, ("seq", "head"))
+        d_normed = lax.psum(normed_part, "head").astype(F32)
+        ffn_out = lax.psum(ffn_part, "head").astype(F32)
+    d_input_norm, _ = norm_back(inputs, scale_one, attn_gain, d_normed)
+    input_grad = d_middle + d_input_norm
+    block_output = (middle + ffn_out).astype(BF16)
     nq, nk, nv = head_count * RQ, head_count * RK, head_count * RV
     cuts = (0, nq, nq + nk, nq + nk + nv)
     query_heads_grad, key_heads_grad, value_heads_grad = [small[i:j].astype(F32).T for i, j in zip(cuts, cuts[1:])]
@@ -1158,7 +1184,7 @@
     return (
         block_output,
         input_grad,
-        small[nq + nk + nv].astype(F32),
+        attn_gain_grad,
         query_heads_grad,
         query_basis_grad,
         key_heads_grad,

time: 419 us -> 409 us (0.976)
  waiting for transfers between devices: 20.6 us -> 0.02 us
  matrix products: 42 us -> 48.6 us
  Pallas kernels: 283 us -> 289 us
    psum x1, waiting for transfers between devices: 20.6 us -> 0.01 us  [shards(): lax.psum(tuple((t.astype(BF16) for t in (gate_grad, up_grad, down_grad)))...]
    pallas_call x1, Pallas kernels: 136 us -> 152 us  [give_back(): pl.pallas_call(functools.partial(return_kernel, rows, packs, chunk, group...]
    dot_general x4 -> x7, matrix products: 9.93 us -> 19.1 us  [weight_grad(): jnp.einsum('rsd,rse->de', normed, grad_rows, preferred_element_type=F32)]
    pallas_call x4 -> x2, Pallas kernels: 14.4 us -> 7.18 us  [pair_sum(): pl.pallas_call(pair_kernel, out_shape=jax.ShapeDtypeStruct(flat.shape, BF...]
    unnamed x122 -> x134, local copies, waits for them, and re-layouts: 21.1 us -> 22.5 us
  transfers between devices with their start and end apart: 1 -> 1, of which waited for: 1 -> 0; matrix products, arithmetic and copies ran while one was open for 9% -> 11% of each run, Pallas kernels for 52% -> 55%
where the time goes in v1:
time: 409 us; the launch traced here: 403 us
  Pallas kernels  289 us (71%)
  matrix products  48.6 us (12%)
  other arithmetic  26.5 us (6%)
  local copies, waits for them, and re-layouts  23.9 us (6%)
  between operations  15.3 us (4%)
    pallas_call x1, Pallas kernels, give_back(): pl.pallas_call(functools.partial(return_kernel, rows, packs, chunk, group...  152 us
    pallas_call x1, Pallas kernels, collect(): pl.pallas_call(functools.partial(collect_kernel, pack_rows, group, block,...  60.3 us
    pallas_call x1, Pallas kernels, weight_sums(): pl.pallas_call(functools.partial(weight_kernel, groups, len(arrays), name...  43.9 us
    unnamed x134, local copies, waits for them, and re-layouts  22.5 us
    pallas_call x1, Pallas kernels, attend_back(): pl.pallas_call(functools.partial(attend_back_kernel, pack_rows, group, bl...  21 us
    dot_general x7, matrix products, weight_grad(): jnp.einsum('rsd,rse->de', normed, grad_rows, preferred_element_type=F32)  19.1 us
    dot_general x9, matrix products, back_project(): jnp.einsum('rse,de->rsd', grad_rows, weight, preferred_element_type=F32)  14.9 us
    dot_general x4, matrix products, project(): jnp.einsum('rsd,de->rse', activations, weight, preferred_element_type=F32)  10 us
  transfers between devices with their start and end apart: 1, of which 0 were waited for; matrix products, arithmetic and copies ran while one was open for 11% of the time, Pallas kernels for 55%

profile of v1, /device:TPU:0, one launch (start us, length us, event | category | flops | bytes accessed | tf_op | source)
XLA Modules:
  0.0 403.2 jit_solution(8113793311712156802)
XLA Ops:
  7.7 1.4 copy-done.2
  9.1 1.1 copy-done.13
  10.3 0.9 copy-done.25
  11.2 0.9 copy-done.27
  12.2 0.9 copy-done.37
  13.0 0.8 copy-done.39
  13.8 0.8 copy-done.41
  14.6 0.7 copy-done.43
  15.2 4.4 %factors.1 = (bf16[12,64,1024]{2,1,0:T(8,128)(2,1)S(1)}, f32[12,64,48]{2,1,0:T(8,128)S(1)}, f32[12,64,384]{2,1,0:T(8,128)S(1)}, bf16[24,64,128]{2,1,0:T(8,128)(2,1)S(1)}, bf16[3,64,128]{2,1,0:T(8,128)(2,1)S(1)}) custom-call(bf16[12,64,1024]{2,1,0:T(8,128)(2,1)S(1)} %copy-done.2, f32[1,1024]{1,0:T(1,128)S(1)} %bitcast.185, bf16[48,1024]{1,0:T(8,128)(2,1)S(1)} %bitcast.178, ...), custom_call_target="tpu_custom_call" | custom-call | tf_op jit(solution)/shard_map/factors/pallas_call | solution.py:139
  19.6 1.2 copy-done.18
  20.8 60.3 %collect.1 = (bf16[27,4,2,2,64,128]{5,4,3,2,1,0:T(8,128)(2,1)S(1)}, f32[12,64,512]{2,1,0:T(8,128)S(1)}, bf16[12,64,512]{2,1,0:T(8,128)(2,1)S(1)}, f32[12,64,128]{2,1,0:T(8,128)S(1)}, bf16[12,64,512]{2,1,0:T(8,128)(2,1)S(1)}) custom-call(s32[12]{0:T(128)S(1)} %copy-done.45, bf16[24,64,128]{2,1,0:T(8,128)(2,1)S(1)} %get-tuple-element.40.kv_ref, ...), custom_call_target="tpu_custom_call" | custom-call | tf_op jit(solution)/shard_map/collect/pallas_call | solution.py:659
  81.1 2.8 copy-done.7
  83.9 1.0 convolution_convert_fusion
  85.0 3.6 pair_sum_4.1
  88.6 0.6 multiply_reduce_fusion
  89.2 0.6 multiply_convert_fusion.3
  89.8 1.2 copy-done.57
  91.0 2.6 fusion.27
  93.9 2.6 fusion.17
  96.5 3.8 multiply_convert_fusion.2
  100.4 3.4 bitcast_convert_fusion.1
  103.8 4.1 %bitcast_convert_fusion = bf16[1024,1408]{1,0:T(8,128)(2,1)} fusion(bf16[12,64,1024]{2,1,0:T(8,128)(2,1)S(1)} %multiply_convert_fusion.3, bf16[12,64,1408]{2,1,0:T(8,128)(2,1)S(1)} %get-tuple-element.74), kind=kOutput, calls=%fused_computation.5 | convolution fusion | flops 2216034304 | bytes 6619136 | tf_op jit(solution)/shard_map/rsd,rse->de/dot_general | solution.py:1025
  107.9 2.4 fusion.16
  110.4 5.9 %fusion.21 = f32[12,64,1024]{2,1,0:T(8,128)} fusion(bf16[12,64,1408]{2,1,0:T(8,128)(2,1)} %copy-done.64, bf16[1024,1408]{1,0:T(8,128)(2,1)S(1)} %copy-done), kind=kOutput, calls=%fused_computation.44 | convolution fusion | flops 2214592512 | bytes 8192000 | tf_op jit(solution)/shard_map/rse,de->rsd/dot_general | solution.py:1021
  116.3 4.3 %fusion.15 = bf16[1408,512]{1,0:T(8,128)(2,1)} fusion(bf16[12,64,1408]{2,1,0:T(8,128)(2,1)} %copy-done.65, bf16[12,64,1024]{2,1,0:T(8,128)(2,1)} %param.29), kind=kOutput, calls=%fused_computation.36 | convolution fusion | flops 1108017152 | bytes 4390912 | tf_op jit(solution)/shard_map/rsd,rse->de/dot_general | solution.py:1025
  120.7 2.8 fusion.29
  123.5 2.6 add_convert_fusion.1
  126.2 3.6 pair_sum_6.1
  129.8 1.7 fusion.5
  131.8 1.3 fusion.39
  133.1 1.9 convolution_convert_fusion.1.do_ref
  135.0 2.0 bitcast_convert_fusion.3
  137.1 3.0 copy-done.8
  140.1 1.4 copy-done.17
  141.6 1.1 copy-done.31
  142.7 1.1 copy-done.32
  143.8 1.0 copy-done.36
  144.9 21.0 %attend_back.1 = (f32[12,64,512]{2,1,0:T(8,128)S(1)}, bf16[24,1024,128]{2,1,0:T(8,128)(2,1)S(1)}, bf16[3,1024,128]{2,1,0:T(8,128)(2,1)S(1)}) custom-call(s32[14]{0:T(128)S(1)} %pad_add_fusion.info_ref, bf16[12,64,512]{2,1,0:T(8,128)(2,1)S(1)} %copy-done.31, bf16[27,1024,128]{2,1,0:T(8,128)(2,1)S(1)} %bitcast.160, bf16[27,1024,128]{2,1,0:T(8,128)(2,1)S(1)} %bitcast.161, ...), custom_call_target="tpu_custom_call" | custom-call | tf_op jit(solution)/shard_map/attend_back/pallas_call | solution.py:411
  166.0 152.1 %give_back.1 = (bf16[12,64,128]{2,1,0:T(8,128)(2,1)S(1)}, bf16[12,64,128]{2,1,0:T(8,128)(2,1)S(1)}, bf16[3,64,128]{2,1,0:T(8,128)(2,1)S(1)}, bf16[12,64,48]{2,1,...) custom-call(bf16[24,4,2,2,64,128]{5,4,3,2,1,0:T(8,128)(2,1)S(1)} %bi, ...), custom_call_target="tpu_custom_call" | custom-call | tf_op jit(solution)/shard_map/give_back/pallas_call | solution.py:766
  318.3 0.6 fusion.59
  319.2 0.5 fusion.66
  319.7 0.5 fusion.61
  320.3 0.6 fusion.52
  320.9 0.6 fusion.54
  321.5 1.6 fusion.88
  323.1 0.5 fusion.36
  323.7 1.4 bitcast_convert_fusion.2
  325.2 0.4 copy-done.60
  325.5 0.7 copy-done.66
  326.2 2.6 fusion.30.refs_3_
  328.8 43.9 %weight_sums.1 = (bf16[2,4,2,48,128]{4,3,2,1,0:T(8,128)(2,1)S(1)}, bf16[2,2,2,4,32,640]{5,4,3,2,1,0:T(8,128)(2,1)S(1)}, bf16[12,64,1024]{2,1,0:T(8,128)(2,1)S(1)...) custom-call(bf16[2,4,2,48,128]{4,3,2,1,0:T(8,128)(2,1)S(1)} %bitcast.175, ...), custom_call_target="tpu_custom_call" | custom-call | tf_op jit(solution)/shard_map/weight_sums/pallas_call | solution.py:992
  372.8 0.6 copy.67
  373.4 0.6 copy.66
  374.1 0.8 fusion.14
  374.9 0.6 slice_convert_fusion.3
  375.5 0.6 fusion.85
  376.1 0.7 bitcast_bitcast_fusion
  376.8 1.0 slice_convert_fusion.1
  377.8 1.2 slice_convert_fusion
  379.1 1.6 bitcast_convert_fusion.4
  380.7 4.0 fusion.13
  384.7 4.9 %convert_element_type.207 = f32[1024,1408]{1,0:T(8,128)} convert(bf16[1024,1408]{1,0:T(8,128)(2,1)} %get-tuple-element.70) | non-fusion elementwise | flops 1441792 | bytes 8650752 | tf_op jit(solution)/shard_map/convert_element_type | solution.py:1155
  389.6 2.9 maximum_convert_fusion
  392.6 3.3 maximum_convert_fusion.1
  (136 shorter events, 1.8 us)
Async XLA Ops:
  7.2 89.3 %copy-start = (bf16[1024,1408]{1,0:T(8,128)(2,1)S(1)}, bf16[1024,1408]{1,0:T(8,128)(2,1)}, u32[]{:S(2)}) copy-start(bf16[1024,1408]{1,0:T(8,128)(2,1)} %param.27) | copy-start | bytes 8650756
  7.2 13.6 %copy-start.45 = (s32[12]{0:T(128)S(1)}, s32[12]{0:T(128)}, u32[]{:S(2)}) copy-start(s32[12]{0:T(128)} %len_ref.1) | copy-start | bytes 148
  7.2 377.5 %all-reduce.4.cloned.1.call-start = ((), (), s32[]{:S(2)}) async-start(), calls=%async_computation | async-start | bytes 12976128 | tf_op jit(solution)/shard_map/psum | solution.py:1155
  7.7 1.4 copy-start.2
  9.1 1.1 copy-start.13
  10.2 0.9 copy-start.25
  11.2 0.9 copy-start.27
  12.2 0.9 copy-start.37
  15.2 68.7 %copy-start.61 = (bf16[512,1024]{1,0:T(8,128)(2,1)S(1)}, bf16[512,1024]{1,0:T(8,128)(2,1)}, u32[]{:S(2)}) copy-start(bf16[512,1024]{1,0:T(8,128)(2,1)} %param.24) | copy-start | bytes 3145732
  19.6 1.2 copy-start.18
  20.8 64.1 %copy-start.11 = (f32[12,64,384]{2,1,0:T(8,128)}, f32[12,64,384]{2,1,0:T(8,128)S(1)}, u32[]{:S(2)}) copy-start(f32[12,64,384]{2,1,0:T(8,128)S(1)} %get-tuple-element.43.bq_ref) | copy-start | bytes 3538948
  20.8 64.1 %copy-start.20 = (f32[12,64,48]{2,1,0:T(8,128)}, f32[12,64,48]{2,1,0:T(8,128)S(1)}, u32[]{:S(2)}) copy-start(f32[12,64,48]{2,1,0:T(8,128)S(1)} %get-tuple-element.42.aq_ref) | copy-start | bytes 442372
  81.1 2.8 copy-start.7
  83.9 4.7 %copy-start.16 = (f32[12,64,512]{2,1,0:T(8,128)}, f32[12,64,512]{2,1,0:T(8,128)S(1)}, u32[]{:S(2)}) copy-start(f32[12,64,512]{2,1,0:T(8,128)S(1)} %get-tuple-element.47.o_ref) | copy-start | bytes 4718596
  83.9 4.7 %copy-start.30 = (bf16[12,64,512]{2,1,0:T(8,128)(2,1)}, bf16[12,64,512]{2,1,0:T(8,128)(2,1)S(1)}, u32[]{:S(2)}) copy-start(bf16[12,64,512]{2,1,0:T(8,128)(2,1)S(1)} %get-tuple-element.45.q_ref) | copy-start | bytes 2359300
  83.9 4.7 %copy-start.35 = (f32[12,64,128]{2,1,0:T(8,128)}, f32[12,64,128]{2,1,0:T(8,128)S(1)}, u32[]{:S(2)}) copy-start(f32[12,64,128]{2,1,0:T(8,128)S(1)} %get-tuple-element.48.lse_ref) | copy-start | bytes 1179652
  83.9 4.7 %copy-start.46 = (bf16[12,64,512]{2,1,0:T(8,128)(2,1)}, bf16[12,64,512]{2,1,0:T(8,128)(2,1)S(1)}, u32[]{:S(2)}) copy-start(bf16[12,64,512]{2,1,0:T(8,128)(2,1)S(1)} %get-tuple-element.44) | copy-start | bytes 2359300
  83.9 4.7 %copy-start.3 = (bf16[12,64,1024]{2,1,0:T(8,128)(2,1)S(1)}, bf16[12,64,1024]{2,1,0:T(8,128)(2,1)}, u32[]{:S(2)}) copy-start(bf16[12,64,1024]{2,1,0:T(8,128)(2,1)} %x_ref.1) | copy-start | bytes 4718596
  84.9 4.3 %copy-start.56 = (f32[1024]{0:T(1024)S(1)}, f32[1024]{0:T(1024)}, u32[]{:S(2)}) copy-start(f32[1024]{0:T(1024)} %param.25) | copy-start | bytes 12292
  88.6 1.2 copy-start.5
  89.2 1.8 copy-start.57
  91.0 12.8 %copy-start.51 = (bf16[12,64,1024]{2,1,0:T(8,128)(2,1)}, bf16[12,64,1024]{2,1,0:T(8,128)(2,1)S(1)}, u32[]{:S(2)}) copy-start(bf16[12,64,1024]{2,1,0:T(8,128)(2,1)S(1)} %multiply_convert_fusion.3) | copy-start | bytes 4718596
  91.0 2.6 copy-start.48
  91.0 2.9 copy-start.59
  100.4 3.4 copy-start.52
  100.4 3.4 copy-start.64
  100.4 7.5 %copy-start.65 = (bf16[12,64,1408]{2,1,0:T(8,128)(2,1)}, bf16[12,64,1408]{2,1,0:T(8,128)(2,1)S(1)}, u32[]{:S(2)}) copy-start(bf16[12,64,1408]{2,1,0:T(8,128)(2,1)S(1)} %get-tuple-element.72) | copy-start | bytes 6488068
  116.3 4.4 %copy-start.53 = (bf16[12,64,1408]{2,1,0:T(8,128)(2,1)S(1)}, bf16[12,64,1408]{2,1,0:T(8,128)(2,1)}, u32[]{:S(2)}) copy-start(bf16[12,64,1408]{2,1,0:T(8,128)(2,1)} %copy-done.52) | copy-start | bytes 6488068
  116.3 7.2 %copy-start.63 = (f32[12,64,1024]{2,1,0:T(8,128)S(1)}, f32[12,64,1024]{2,1,0:T(8,128)}, u32[]{:S(2)}) copy-start(f32[12,64,1024]{2,1,0:T(8,128)} %fusion.21) | copy-start | bytes 9437188
  120.7 2.8 copy-start.58
  126.1 3.6 copy-start.4
  126.1 3.6 copy-start.6
  129.8 3.3 copy-start.9
  129.8 2.0 copy-start.49
  131.8 1.3 copy-start.62
  133.1 1.9 copy-start.47
  137.1 3.1 copy-start.8
  140.1 1.4 copy-start.17
  141.6 1.1 copy-start.31
  142.7 1.1 copy-start.32
  143.8 1.0 copy-start.36
  144.9 21.0 %copy-start.12 = (f32[12,64,384]{2,1,0:T(8,128)S(1)}, f32[12,64,384]{2,1,0:T(8,128)}, u32[]{:S(2)}) copy-start(f32[12,64,384]{2,1,0:T(8,128)} %copy-done.11) | copy-start | bytes 3538948
  144.9 21.1 %copy-start.15 = (bf16[256,1408]{1,0:T(8,128)(2,1)S(1)}, bf16[256,1408]{1,0:T(8,128)(2,1)}, u32[]{:S(2)}) copy-start(bf16[256,1408]{1,0:T(8,128)(2,1)} %fusion.29) | copy-start | bytes 2162692
  144.9 21.1 %copy-start.21 = (f32[12,64,48]{2,1,0:T(8,128)S(1)}, f32[12,64,48]{2,1,0:T(8,128)}, u32[]{:S(2)}) copy-start(f32[12,64,48]{2,1,0:T(8,128)} %copy-done.20) | copy-start | bytes 442372
  144.9 21.1 %copy-start.24 = (bf16[1408,512]{1,0:T(8,128)(2,1)S(1)}, bf16[1408,512]{1,0:T(8,128)(2,1)}, u32[]{:S(2)}) copy-start(bf16[1408,512]{1,0:T(8,128)(2,1)} %fusion.15) | copy-start | bytes 4325380
  144.9 21.1 %copy-start.29 = (bf16[512,1024]{1,0:T(8,128)(2,1)S(1)}, bf16[512,1024]{1,0:T(8,128)(2,1)}, u32[]{:S(2)}) copy-start(bf16[512,1024]{1,0:T(8,128)(2,1)} %bitcast_convert_fusion.3) | copy-start | bytes 3145732
  165.9 152.3 %copy-start.40 = (bf16[1024,16]{0,1:T(8,128)(2,1)S(1)}, bf16[1024,16]{0,1:T(8,128)(2,1)}, u32[]{:S(2)}) copy-start(bf16[1024,16]{0,1:T(8,128)(2,1)} %param.22) | copy-start | bytes 98308
  318.1 1.6 copy-start.22
  318.1 1.1 copy-start.38
  318.3 1.4 copy-start.42
  319.1 1.2 copy-start.26
  319.7 1.2 copy-start.28
  320.3 1.2 copy-start.14
  321.5 1.6 copy-start.19
  323.7 1.8 copy-start.60
  323.7 2.5 copy-start.66
  328.8 45.3 %copy-start.44 = (f32[1024]{0:T(1024)S(1)}, f32[1024]{0:T(1024)}, u32[]{:S(2)}) copy-start(f32[1024]{0:T(1024)} %param.17) | copy-start | bytes 12292
  377.8 2.9 copy-start.10
  377.8 2.9 copy-start.50
  384.7 4.9 %copy-start.34 = (bf16[2,2,4,16,1408]{4,3,2,1,0:T(8,128)(2,1)S(1)}, bf16[2,2,4,16,1408]{4,3,2,1,0:T(8,128)(2,1)}, u32[]{:S(2)}) copy-start(bf16[2,2,4,16,1408]{4,3,2,1,0:T(8,128)(2,1)} %copy-done.33) | copy-start | bytes 2162692
  384.7 4.9 %copy-start.54 = (bf16[768,1408]{1,0:T(8,128)(2,1)S(1)}, bf16[768,1408]{1,0:T(8,128)(2,1)}, u32[]{:S(2)}) copy-start(bf16[768,1408]{1,0:T(8,128)(2,1)} %get-tuple-element.69) | copy-start | bytes 6488068
  389.6 2.9 copy-start.23
  389.6 3.0 copy-start.55
  392.5 3.4 copy-start.1
  (4 other events, 3.1 us)
Sparse Core Ops, SparseCore 0:
  110.5 272.2 all-reduce.3
